TPU v7x, 128 devices: a whole 4x4x4 slice. The times are simulated.
128 devices in a mesh: grp: 4 (over z), dev: 32 (over x, y, core).
Axes of the slice: x: 4, y: 4, z: 4, core: 2. Of those that a mesh axis runs over, the one named last changes fastest.
Arguments:
- head_emb: bfloat16 [131072, 400], P(('grp', 'dev')), may hold values from -2 to 2
- tail_emb: bfloat16 [131072, 400], P(('grp', 'dev')), may hold values from -2 to 2
- relation: int32 [131072], P(('grp', 'dev')), may hold values from 0 to 14823
- owners: int32 [131072, 2], P(('grp', 'dev')), may hold values from 0 to 127, all different within a row; in each aligned block of 1024 rows (0 to 1023, 1024 to 2047, ...) at most 32 rows name the same one
- owner_rows: int32 [131072, 2], P(('grp', 'dev')), may hold values from 0 to 4095
- entities: bfloat16 [524288, 400], P(('grp', 'dev')), may hold values from -2 to 2
- neg_rows: int32 [1, 16384], P(None, ('grp', 'dev')), may hold values from 0 to 4095
- coef: float32 [14824, 100], replicated, may hold values from -4 to 4
- bases: float32 [100, 400], replicated, may hold values from -0.625 to 0.625
Outputs:
- ent_grad: float32 [524288, 400], P(('grp', 'dev'))
- coef_grad: float32 [14824, 100], replicated
- bases_grad: float32 [100, 400], replicated
Inputs may be any that keep to these rules, and one draw needn't show every extreme that they name: The two owners of a row differ; within the triples of one device no owner is named by more than 32 entries of both columns together.
All inputs are finite; a program needn't handle non-finite values.
Results may differ from a plain program's by a relative error of at most 0.0029.
Values may be sent and summed in bfloat16 or wider, within the bound.
A program may use at most 128 MiB of HBM per device.

v0:
```python
import jax
import jax.numpy as jnp
from jax import lax
from jax.sharding import PartitionSpec as P


def per_device(head_emb, tail_emb, relation, owners, owner_rows, entities, neg_rows, coef, bases):
    highest = lax.Precision.HIGHEST
    triple_count, columns = head_emb.shape
    block_count, neg_local = neg_rows.shape
    group_size = lax.axis_size("dev")
    all_devices = lax.axis_size("grp") * group_size
    neg_count = neg_local * group_size
    ent_local = entities.shape[0]
    picked = coef[relation]
    rel_vec = jnp.dot(picked, bases, precision=highest)
    local_negs = entities[neg_rows]
    group_negs = lax.all_gather(local_negs, "dev", axis=1, tiled=True)
    head_f = head_emb.astype(jnp.float32)
    tail_f = tail_emb.astype(jnp.float32)
    head_rel = (head_f * rel_vec).astype(jnp.bfloat16)
    number = 0
    negatives = group_negs[number]
    scores = lax.dot_general(
        head_rel, negatives, (((1,), (1,)), ((), ())), preferred_element_type=jnp.float32
    )
    neg_prob = jax.nn.sigmoid(scores).astype(jnp.bfloat16)
    probs_list = [neg_prob]
    mix_list = jnp.dot(neg_prob, negatives, preferred_element_type=jnp.float32)
    number = 0
    probs_part = probs_list[number]
    pieces = [
        lax.dot_general(
            probs_part, head_rel, (((0,), (0,)), ((), ())), preferred_element_type=jnp.float32
        )
        / neg_count
    ]
    own_neg = lax.psum_scatter(
        jnp.stack(pieces, axis=1).astype(jnp.bfloat16), "dev", scatter_dimension=0, tiled=True
    ).astype(jnp.float32)
    pos_gate = jax.nn.sigmoid(-jnp.sum(head_f * rel_vec * tail_f, axis=1))[:, None]
    head_grad = (-pos_gate * rel_vec * tail_f + rel_vec * mix_list / neg_count).astype(jnp.bfloat16)
    tail_grad = (-pos_gate * head_f * rel_vec).astype(jnp.bfloat16)
    rel_grad = -pos_gate * head_f * tail_f + head_f * mix_list / neg_count
    ent_grad = jnp.zeros((ent_local, columns), jnp.float32)
    ent_grad = ent_grad.at[neg_rows.T.reshape(-1)].add(own_neg.reshape(-1, columns))
    capacity = 4 * triple_count // all_devices
    grad_rows = jnp.stack([head_grad, tail_grad], axis=1).reshape(2 * triple_count, columns)
    target_dev = owners.reshape(-1)
    entry_rows = owner_rows.reshape(-1)
    onehot = (target_dev[:, None] == jnp.arange(all_devices, dtype=jnp.int32)[None, :]).astype(
        jnp.int32
    )
    slot_index = jnp.sum(jnp.cumsum(onehot, axis=0) * onehot, axis=1) - 1
    position = target_dev * capacity + slot_index
    send_rows = (
        jnp.zeros((all_devices * capacity, columns), jnp.bfloat16).at[position].set(grad_rows)
    )
    send_index = jnp.zeros((all_devices * capacity,), jnp.int32).at[position].set(entry_rows)
    recv_rows, recv_index = (
        lax.all_to_all(send_rows, ("grp", "dev"), split_axis=0, concat_axis=0, tiled=True),
        lax.all_to_all(send_index, ("grp", "dev"), split_axis=0, concat_axis=0, tiled=True),
    )
    ent_grad = ent_grad.at[recv_index].add(recv_rows.astype(jnp.float32))
    coef_rows = jnp.dot(rel_grad, bases.T, precision=highest)
    coef_local = jax.ops.segment_sum(coef_rows, relation, num_segments=coef.shape[0])
    bases_local = jnp.dot(picked.T, rel_grad, precision=highest)
    coef_grad, bases_grad = lax.psum((coef_local, bases_local), ("grp", "dev"))
    return (ent_grad, coef_grad, bases_grad)


def solution(mesh):
    return jax.shard_map(
        per_device,
        mesh=mesh,
        in_specs=(
            P(("grp", "dev"), None),
            P(("grp", "dev"), None),
            P(("grp", "dev")),
            P(("grp", "dev"), None),
            P(("grp", "dev"), None),
            P(("grp", "dev"), None),
            P(None, ("grp", "dev")),
            P(),
            P(),
        ),
        out_specs=(P(("grp", "dev"), None), P(), P()),
        check_vma=False,
    )
```

profile of v0, /device:TPU:1, one launch (start us, length us, event | category | flops | bytes accessed | tf_op | source)
XLA Modules:
  0.0 422.2 jit_solution(1812944348020675076)
XLA Ops:
  7.2 6.0 %copy.28 = bf16[4096,400]{1,0:T(8,128)(2,1)} copy(bf16[4096,400]{0,1:T(8,128)(2,1)} %param.14) | data formatting | bytes 6553600 | tf_op args[5]
  13.3 4.3 %gather_fusion.1 = bf16[128,400]{1,0:T(8,128)(2,1)} fusion(bf16[4096,400]{1,0:T(8,128)(2,1)} %copy.28, s32[1024]{0:T(1024)S(1)} %pad_clamp_fusion), kind=kCustom, calls=%fused_computation.1 | custom fusion | bytes 205312 | tf_op jit(solution)/shard_map/gather | solution.py:17
  17.6 8.2 %copy.27 = f32[14824,100]{1,0:T(8,128)} copy(f32[14824,100]{0,1:T(8,128)} %param.16) | data formatting | bytes 11859200 | tf_op args[7]
  25.8 7.3 %gather_fusion = f32[1024,100]{1,0:T(8,128)} fusion(f32[14824,100]{1,0:T(8,128)} %copy.27, s32[1024]{0:T(1024)S(1)} %fusion.28), kind=kCustom, calls=%fused_computation | custom fusion | bytes 823296 | tf_op jit(solution)/shard_map/gather | solution.py:15
  33.1 2.8 fusion.12
  35.9 31.3 %all-gather.3.cloned.1.call-done = bf16[4096,400]{1,0:T(8,128)(2,1)} async-done(((bf16[128,400]{1,0:T(8,128)(2,1)}), bf16[4096,400]{1,0:T(8,128)(2,1)}) %all-gather.3.cloned.1.call-update) | async-done | bytes 3276816 | tf_op jit(solution)/shard_map/all_gather | solution.py:18
  67.3 9.9 %divide_convert_fusion = bf16[1024,4096]{1,0:T(8,128)(2,1)S(1)} fusion(bf16[4096,400]{1,0:T(8,128)(2,1)} %all-gather.3.cloned.1.call-done, f32[1024,400]{0,1:T(8,128)S(1)} %get-tuple-element.14, bf16[1024,400]{0,1:T(8,128)(2,1)S(1)} %copy-done.3), kind=kOutput, calls=%fused_computation.7 | convolution fusion | flops 3373449216 | bytes 14123008 | tf_op jit(solution)/shard_map/dot_general | solution.py:24
  77.2 3.7 fusion.35
  83.2 4.4 %fusion.24 = f32[1024,100]{1,0:T(8,128)} fusion(f32[100,400]{0,1:T(8,128)S(1)} %copy-done, f32[1024,400]{0,1:T(8,128)S(1)} %fusion.35, bf16[1024,400]{0,1:T(8,128)(2,1)S(1)} %copy-done.3, bf16[1024,400]{0,1:T(8,128)(2,1)S(1)} %copy-done.2, f32[1024]{0:T(1024)S(1)} %divide_negate_fusion), kind=kOutput, calls=%fused_computation.43 | convolution fusion | flops 494387200 | bytes 3850496 | tf_op jit(solution)/shard_map/dot_general | solution.py:65
  87.6 9.9 %scatter_custom_fusion.4 = f32[14824,100]{1,0:T(8,128)} fusion(s32[1024]{0:T(1024)S(1)} %copy-done.11, f32[1024,100]{1,0:T(8,128)} %fusion.24, f32[]{:T(128)} %constant.9.clone.1), kind=kCustom, calls=%fused_computation.13 | custom fusion | flops 102400 | bytes 5930112 | tf_op jit(solution)/shard_map/scatter-add | solution.py:66
  102.1 9.9 %multiply_convert_fusion = bf16[4096,400]{0,1:T(8,128)(2,1)} fusion(bf16[1024,4096]{1,0:T(8,128)(2,1)} %copy-done.14, f32[1024,400]{0,1:T(8,128)} %copy-done.4, bf16[1024,400]{0,1:T(8,128)(2,1)S(1)} %copy-done.3), kind=kOutput, calls=%fused_computation.10 | convolution fusion | flops 3359948800 | bytes 14123008 | tf_op jit(solution)/shard_map/dot_general | solution.py:33
  111.9 6.0 %copy.44 = bf16[4096,400]{1,0:T(8,128)(2,1)} copy(bf16[4096,400]{0,1:T(8,128)(2,1)} %multiply_convert_fusion) | data formatting | bytes 6553600
  131.6 8.1 %scatter_custom_fusion.1 = s32[4096]{0:T(1024)S(1)} fusion(s32[2048]{0:T(1024)S(1)} %bitcast.45, s32[2048]{0:T(1024)S(1)} %reshape.175, s32[]{:T(128)} %constant.10.clone.1), kind=kCustom, calls=%fused_computation.48 | custom fusion | bytes 16388 | tf_op jit(solution)/shard_map/scatter | solution.py:59
  140.4 6.6 %all-to-all-start = ((s32[128,32,1]{1,2,0:T(1,128)}), s32[128,32,1]{1,2,0:T(1,128)S(1)}, u32[]{:S(2)}, u32[]{:S(2)}) async-start(s32[128,32,1]{1,2,0:T(1,128)} %bitcast.10), calls=%async_computation | async-start | bytes 131072 | tf_op jit(solution)/shard_map/all_to_all | solution.py:62
  150.5 4.8 %copy.37 = bf16[1024,2,400]{2,1,0:T(2,128)(2,1)S(1)} copy(bf16[1024,2,400]{0,2,1:T(8,128)(2,1)} %pad_maximum_fusion) | data formatting | bytes 3276800 | tf_op jit(solution)/shard_map/stack | solution.py:48
  155.2 2.9 reshape.183
  158.1 12.8 %scatter_custom_fusion.2 = bf16[4096,400]{1,0:T(8,128)(2,1)} fusion(s32[2048]{0:T(1024)S(1)} %bitcast.46, bf16[2048,400]{1,0:T(8,128)(2,1)} %reshape.183, bf16[]{:T(256)} %constant.17.clone.1), kind=kCustom, calls=%fused_computation.21 | custom fusion | bytes 3277312 | tf_op jit(solution)/shard_map/scatter | solution.py:57
  171.0 10.2 %all-to-all-start.1 = ((bf16[128,32,400]{2,1,0:T(8,128)(2,1)}), bf16[128,32,400]{2,1,0:T(8,128)(2,1)}, u32[]{:S(2)}, u32[]{:S(2)}) async-start(bf16[128,32,400]{2,1,0:T(8,128)(2,1)} %bitcast.42), calls=%async_computation.1 | async-start | bytes 8388608 | tf_op jit(solution)/shard_map/all_to_all | solution.py:61
  182.7 100.8 %all-reduce.3.cloned.1.call-done = (f32[14824,100]{1,0:T(8,128)}, f32[100,400]{0,1:T(8,128)}) async-done(((f32[14824,100]{1,0:T(8,128)}, f32[100,400]{0,1:T(8,128)}), (f32[14824,100]{1,0:T(8,128)}, f32[100,400]{0,1:T(8,128)})) %all-reduce.3.cloned.1.call-update) | async-done | bytes 6089616 | tf_op jit(solution)/shard_map/psum | solution.py:68
  283.5 8.5 %copy.40 = f32[14824,100]{0,1:T(8,128)} copy(f32[14824,100]{1,0:T(8,128)} %get-tuple-element.9) | data formatting | bytes 11859200
  292.0 74.8 %reduce-scatter.4.cloned.1.call-done = bf16[128,400]{1,0:T(8,128)(2,1)} async-done(((bf16[4096,400]{1,0:T(8,128)(2,1)}), bf16[128,400]{1,0:T(8,128)(2,1)}) %reduce-scatter.4.cloned.1.call-update) | async-done | bytes 102416
  367.9 5.0 %scatter_custom_fusion = f32[4096,400]{1,0:T(8,128)} fusion(s32[128]{0:T(128)S(1)} %fusion.29, f32[128,400]{1,0:T(8,128)S(1)} %copy.29, f32[]{:T(128)} %constant.9.clone.1), kind=kCustom, calls=%fused_computation.11 | custom fusion | flops 51200 | bytes 6553604 | tf_op jit(solution)/shard_map/scatter-add | solution.py:46
  372.9 33.3 %scatter_custom_fusion.3 = f32[4096,400]{1,0:T(8,128)} fusion(f32[4096,400]{1,0:T(8,128)} %scatter_custom_fusion, s32[4096]{0:T(1024)S(1)} %bitcast.44, bf16[4096,400]{1,0:T(8,128)(2,1)} %bitcast.21), kind=kCustom, calls=%fused_computation.8 | custom fusion | flops 3276800 | bytes 10747904 | tf_op jit(solution)/shard_map/scatter-add | solution.py:64
  406.2 8.6 %copy.39 = f32[4096,400]{0,1:T(8,128)} copy(f32[4096,400]{1,0:T(8,128)} %scatter_custom_fusion.3) | data formatting | bytes 13107200
  (73 shorter events, 28.0 us)
Async XLA Ops:
  7.2 25.9 %copy-start = (f32[100,400]{0,1:T(8,128)S(1)}, f32[100,400]{0,1:T(8,128)}, u32[]{:S(2)}) copy-start(f32[100,400]{0,1:T(8,128)} %param.17) | copy-start | bytes 480004
  7.2 6.1 %copy-start.13 = (s32[1,128]{1,0:T(1,128)S(1)}, s32[1,128]{1,0:T(1,128)}, u32[]{:S(2)}) copy-start(s32[1,128]{1,0:T(1,128)} %param.15) | copy-start | bytes 1540
  7.2 60.1 %all-gather.3.cloned.1.call-start = ((), (), s32[]{:S(2)}) async-start(), calls=%async_computation.3 | async-start | bytes 4325376 | tf_op jit(solution)/shard_map/all_gather | solution.py:18
  17.5 8.2 %copy-start.11 = (s32[1024]{0:T(1024)S(1)}, s32[1024]{0:T(1024)}, u32[]{:S(2)}) copy-start(s32[1024]{0:T(1024)} %param.11) | copy-start | bytes 12292
  17.5 265.9 %all-reduce.3.cloned.1.call-start = ((), (), s32[]{:S(2)}) async-start(), calls=%async_computation.5 | async-start | bytes 15589376 | tf_op jit(solution)/shard_map/psum | solution.py:68
  25.8 7.3 %copy-start.2 = (bf16[1024,400]{0,1:T(8,128)(2,1)S(1)}, bf16[1024,400]{0,1:T(8,128)(2,1)}, u32[]{:S(2)}) copy-start(bf16[1024,400]{0,1:T(8,128)(2,1)} %param.10) | copy-start | bytes 2457604
  25.8 7.3 %copy-start.3 = (bf16[1024,400]{0,1:T(8,128)(2,1)S(1)}, bf16[1024,400]{0,1:T(8,128)(2,1)}, u32[]{:S(2)}) copy-start(bf16[1024,400]{0,1:T(8,128)(2,1)} %param.9) | copy-start | bytes 2457604
  35.9 31.4 %copy-start.4 = (f32[1024,400]{0,1:T(8,128)}, f32[1024,400]{0,1:T(8,128)S(1)}, u32[]{:S(2)}) copy-start(f32[1024,400]{0,1:T(8,128)S(1)} %get-tuple-element.14) | copy-start | bytes 4915204
  67.3 9.9 %copy-start.12 = (bf16[4096,400]{1,0:T(8,128)(2,1)S(1)}, bf16[4096,400]{1,0:T(8,128)(2,1)}, u32[]{:S(2)}) copy-start(bf16[4096,400]{1,0:T(8,128)(2,1)} %all-gather.3.cloned.1.call-done) | copy-start | bytes 9830404
  77.1 3.7 copy-start.14
  77.2 3.7 copy-start.5
  97.5 0.7 copy-start.9
  97.5 269.2 %reduce-scatter.4.cloned.1.call-start = ((), (), s32[]{:S(2)}) async-start(), calls=%async_computation.4 | async-start | bytes 4325376
  101.1 1.0 copy-start.6
  102.1 9.9 %copy-start.8 = (s32[128,17]{0,1:T(8,128)}, s32[128,17]{0,1:T(8,128)S(1)}, u32[]{:S(2)}) copy-start(s32[128,17]{0,1:T(8,128)S(1)} %reduce-window.9) | copy-start | bytes 26116
  118.0 0.7 slice-start
  118.7 8.6 %copy-start.10 = (s32[1024,2]{0,1:T(2,128)S(1)}, s32[1024,2]{0,1:T(2,128)}, u32[]{:S(2)}) copy-start(s32[1024,2]{0,1:T(2,128)} %param.13) | copy-start | bytes 24580
  140.4 30.6 %all-to-all-start = ((s32[128,32,1]{1,2,0:T(1,128)}), s32[128,32,1]{1,2,0:T(1,128)S(1)}, u32[]{:S(2)}, u32[]{:S(2)}) async-start(s32[128,32,1]{1,2,0:T(1,128)} %bitcast.10), calls=%async_computation | async-start | bytes 131072 | tf_op jit(solution)/shard_map/all_to_all | solution.py:62
  171.0 202.0 %all-to-all-start.1 = ((bf16[128,32,400]{2,1,0:T(8,128)(2,1)}), bf16[128,32,400]{2,1,0:T(8,128)(2,1)}, u32[]{:S(2)}, u32[]{:S(2)}) async-start(bf16[128,32,400]{2,1,0:T(8,128)(2,1)} %bitcast.42), calls=%async_computation.1 | async-start | bytes 8388608 | tf_op jit(solution)/shard_map/all_to_all | solution.py:61
  406.2 8.6 %copy-start.7 = (f32[100,400]{0,1:T(8,128)S(1)}, f32[100,400]{0,1:T(8,128)}, u32[]{:S(2)}) copy-start(f32[100,400]{0,1:T(8,128)} %get-tuple-element.17) | copy-start | bytes 480004
  406.2 9.3 %copy-start.1 = (f32[100,400]{0,1:T(8,128)S(1)}, f32[100,400]{0,1:T(8,128)}, u32[]{:S(2)}) copy-start(f32[100,400]{0,1:T(8,128)} %param.17) | copy-start | bytes 480004
Sparse Core Ops, SparseCore 0:
  17.7 49.5 all-gather.2
  97.7 185.7 all-reduce.2
  288.1 78.5 reduce-scatter.3
where the time goes:
time: 430 us; the launch traced here: 422 us
  waiting for transfers between devices  207 us (48%)
  local copies, waits for them, and re-layouts  93.8 us (22%)
  other arithmetic  57.2 us (13%)
  matrix products  32.9 us (8%)
  starting transfers between devices  17.1 us (4%)
  between operations  14.2 us (3%)
    psum x1, waiting for transfers between devices, per_device(): coef_grad, bases_grad = lax.psum((coef_local, bases_local), ('grp', 'dev'))  101 us
    unnamed x4, waiting for transfers between devices  74.8 us
    unnamed x39, local copies, waits for them, and re-layouts  42.6 us
    scatter-add x1, other arithmetic, per_device(): ent_grad = ent_grad.at[recv_index].add(recv_rows.astype(jnp.float32))  33.3 us
    all_gather x1, waiting for transfers between devices, per_device(): group_negs = lax.all_gather(local_negs, 'dev', axis=1, tiled=True)  31.3 us
    scatter x1, local copies, waits for them, and re-layouts, per_device(): jnp.zeros((all_devices * capacity, columns), jnp.bfloat16).at[position]  12.8 us
    all_to_all x1, starting transfers between devices, per_device(): lax.all_to_all(send_rows, ('grp', 'dev'), split_axis=0, concat_axis=0, ti...  10.2 us
    scatter-add x1, other arithmetic, per_device(): jax.ops.segment_sum(coef_rows, relation, num_segments=coef.shape[0])  9.93 us
  transfers between devices with their start and end apart: 5, of which 3 were waited for; matrix products, arithmetic and copies ran while one was open for 23% of the time, Pallas kernels for 0%

commit v1 on v0

v1 whole, which is shorter than its diff:
```python
import functools

import jax
import jax.numpy as jnp
from jax import lax
from jax.experimental import pallas as pl
from jax.experimental.pallas import tpu as pltpu
from jax.sharding import PartitionSpec as P

MESH = pl.DeviceIdType.MESH
HIGHEST = lax.Precision.HIGHEST
D = 400
NB = 100
TRIP = 1024
NEG = 128
ENT = 4096
NREL = 14824
GROUP = 32
NEG_ALL = NEG * GROUP
RA = (0, 208)
RB = (208, 192)
LOROW = 112
VM = pl.BlockSpec(memory_space=pltpu.VMEM)
ANY = pl.BlockSpec(memory_space=pl.ANY)
BF = jnp.bfloat16
F32 = jnp.float32


def dot(a, b, ca=1, cb=0, precision=None):
    return lax.dot_general(
        a, b, (((ca,), (cb,)), ((), ())), preferred_element_type=F32, precision=precision
    )


def spread(ids, rows):
    return (lax.broadcasted_iota(jnp.int32, (rows, ids.shape[1]), 0) == ids).astype(F32).astype(BF)


def equals(ids, value):
    return (ids == value).astype(F32).astype(BF)


def score_kernel(
    head, tail, rel, owners, negr, basest, coeft, entt,
    own_neg, grads, rows, bases_part, pos,
    coefv, entv, st, oh, pk, picked, relv, hrt, hr, mix, got, grd, pair, r2a, r2b, s3a, s3b, r3, blk,
    ss, rs, loc,
):
    g, k = lax.axis_index("grp"), lax.axis_index("dev")
    x, y, c = k // 8, lax.rem(k // 2, 4), lax.rem(k, 2)

    def dev(dx, dy, dc):
        return (g, (lax.rem(x + dx, 4) * 4 + lax.rem(y + dy, 4)) * 2 + lax.rem(c + dc, 2))

    get_ent = pltpu.make_async_copy(entt, entv, loc.at[0])
    get_ent.start()
    get_coef = pltpu.make_async_copy(coeft, coefv, loc.at[1])
    get_coef.start()
    bar = pltpu.get_barrier_semaphore()
    XP = [dev(d, 0, 0) for d in (1, 2, 3)]
    YP = [dev(0, d, 0) for d in (1, 2, 3)]
    CP = dev(0, 0, 1)
    for p in XP + YP + [CP]:
        pl.semaphore_signal(bar, inc=1, device_id=p, device_id_type=MESH)
    count = [0]
    sent = []

    def send(src, dst, p):
        i = count[0]
        count[0] += 1
        cp = pltpu.make_async_remote_copy(
            src_ref=src, dst_ref=dst, send_sem=ss.at[i], recv_sem=rs.at[i], device_id=p, device_id_type=MESH
        )
        cp.start()
        sent.append(cp)
        return cp

    pick_neg = spread(negr[...], ENT)
    get_ent.wait()
    got[c, y, x] = dot(entv[...], pick_neg).astype(BF)
    pl.semaphore_wait(bar, 7)
    A, B = pl.ds(*RA), pl.ds(*RB)
    mine_a, mine_b = got.at[c, y, x, A], got.at[c, y, x, B]
    a1 = [send(mine_a, mine_a, XP[d]) for d in (1, 0, 2)]
    b1 = [send(mine_b, mine_b, YP[d]) for d in (1, 0, 2)]

    st[...] = jnp.zeros_like(st)
    pk[...] = jnp.zeros_like(pk)
    ids = rel[...]
    low = spread(ids & 255, 256)
    high = lax.shift_right_logical(ids, 8)
    get_coef.wait()

    def load_coef(base, width, at):
        part = coefv[:, pl.ds(base, width)]
        first = part.astype(BF)
        st[0:NB, at : at + width] = first
        st[LOROW : LOROW + NB, at : at + width] = (part - first.astype(F32)).astype(BF)

    def gather(step):
        base = pl.multiple_of(step * 1024, 1024)
        load_coef(base, 1024, 0)
        for q in range(4):
            oh[q * 256 : (q + 1) * 256, :] = low * equals(high, step * 4 + q)
        pk[...] += dot(st[...], oh[...])

    def gather_loop(start, stop):
        def body(i, carry):
            gather(i)
            return carry

        lax.fori_loop(start, stop, body, 0)

    gather_loop(0, 5)
    for cp in a1:
        cp.wait_recv()
    line_a = got.at[c, y, :, A]
    a2 = [send(line_a, line_a, YP[d]) for d in (1, 0, 2)]
    for cp in b1:
        cp.wait_recv()
    line_b = got.at[c, :, x, B]
    b2 = [send(line_b, line_b, XP[d]) for d in (1, 0, 2)]
    last = [send(line_a, line_a, CP), send(line_b, line_b, CP)]

    gather_loop(5, 14)
    full = NREL // 1024 * 1024
    rest = NREL - full - 256
    load_coef(full, 256, 0)
    load_coef(full + 256, rest, 256)
    for q in range(2):
        oh[q * 256 : (q + 1) * 256, :] = low * equals(high, full // 256 + q)
    pk[...] += dot(st[:, 0 : 256 + rest], oh[0 : 256 + rest, :])
    chosen = pk[0:NB] + pk[LOROW : LOROW + NB]
    picked[...] = chosen
    relv[...] = dot(basest[...], chosen, precision=HIGHEST)
    hb = (head[...].astype(F32) * relv[...]).astype(BF)
    hrt[...] = hb
    hr[...] = hb.T
    tri = (
        lax.broadcasted_iota(jnp.int32, (256, 256), 0) < lax.broadcasted_iota(jnp.int32, (256, 256), 1)
    ).astype(F32).astype(BF)
    before = jnp.zeros((128, 1), F32)
    for h in range(2):
        for b in range(4):
            o = owners[h : h + 1, b * 256 : (b + 1) * 256]
            one = spread(o, 128)
            onef = one.astype(F32)
            rank = jnp.sum((dot(one, tri) + before) * onef, axis=0, keepdims=True)
            before = before + jnp.sum(onef, axis=1, keepdims=True)
            pos[h : h + 1, b * 256 : (b + 1) * 256] = o * 32 + rank.astype(jnp.int32)

    for j, d in ((1, 1), (2, 3), (0, 2)):
        a2[j].wait_recv()
        r = got.at[c, lax.rem(y - d + 4, 4), :, A]
        last.append(send(r, r, CP))
        b2[j].wait_recv()
        r = got.at[c, :, lax.rem(x - d + 4, 4), B]
        last.append(send(r, r, CP))
    for cp in last:
        cp.wait_recv()

    mix[...] = jnp.zeros_like(mix)

    def chunk(cc, yy):
        for q in range(4):
            blk[:, q * 128 : (q + 1) * 128] = got[cc, yy, q]
        n = blk[...]
        s = dot(hr[...], n)
        prob = (0.5 * jnp.tanh(0.5 * s) + 0.5).astype(BF)
        mix[...] += dot(n, prob, 1, 1)
        part = (dot(hrt[...], prob) * (1.0 / NEG_ALL)).astype(BF)
        for q in range(4):
            grd[cc, yy, q] = part[:, q * 128 : (q + 1) * 128]

    halves = []
    for s in range(4):
        yy = lax.rem(y + 1 + s, 4)
        chunk(1 - c, yy)
        halves.append(send(grd.at[1 - c, yy], pair.at[yy], CP))
    a4, b4 = [], []
    for s in range(4):
        yy = lax.rem(y + 1 + s, 4)
        chunk(c, yy)
        halves[s].wait_recv()
        grd[c, yy] = (grd[c, yy].astype(F32) + pair[yy].astype(F32)).astype(BF)
        if s < 3:
            a4.append(send(grd.at[c, yy, :, A], r2a.at[s], YP[s]))
        for d in (1, 2, 3):
            xx = lax.rem(x + d, 4)
            b4.append(send(grd.at[c, yy, xx, B], r2b.at[d - 1, yy], XP[d - 1]))

    h, t = head[...].astype(F32), tail[...].astype(F32)
    rv = relv[...]
    hrv = h * rv
    score = jnp.sum(hrv * t, axis=0, keepdims=True)
    gate = 0.5 - 0.5 * jnp.tanh(0.5 * score)
    mean = mix[...] * (1.0 / NEG_ALL)
    inner = mean - gate * t
    grads[0] = (rv * inner).astype(BF)
    grads[1] = (-gate * hrv).astype(BF)
    rg = h * inner

    for cp in a4:
        cp.wait_recv()
    tot = grd[c, y, :, 0:208, :].astype(F32)
    for d in range(3):
        tot += r2a[d].astype(F32)
    s3a[...] = tot.astype(BF)
    a5 = [send(s3a.at[lax.rem(x + d, 4)], r3.at[d - 1, A], XP[d - 1]) for d in (1, 2, 3)]
    for cp in b4:
        cp.wait_recv()
    tot = grd[c, :, x, 208:400, :].astype(F32)
    for d in range(3):
        tot += r2b[d].astype(F32)
    s3b[...] = tot.astype(BF)
    b5 = [send(s3b.at[lax.rem(y + d, 4)], r3.at[d - 1, B], YP[d - 1]) for d in (1, 2, 3)]

    crow = dot(basest[...], rg, 0, 0, precision=HIGHEST)
    first = crow.astype(BF)
    rows[...] = jnp.zeros_like(rows)
    rows[0:NB] = first
    rows[LOROW : LOROW + NB] = (crow - first.astype(F32)).astype(BF)
    bases_part[...] = jnp.zeros_like(bases_part)
    bases_part[0:D, 0:NB] = dot(rg, picked[...], 1, 1, precision=HIGHEST)

    for cp in a5:
        cp.wait_recv()
    tot = s3a[x].astype(F32)
    for d in range(3):
        tot += r3[d, 0:208].astype(F32)
    own_neg[0:208] = tot
    for cp in b5:
        cp.wait_recv()
    tot = s3b[y].astype(F32)
    for d in range(3):
        tot += r3[d, 208:400].astype(F32)
    own_neg[208:400] = tot
    for cp in sent:
        cp.wait_send()


def score(head, tail, rel, owners, negr, basest, coeft, entt):
    sem = pltpu.SemaphoreType.DMA
    v = pltpu.VMEM
    return pl.pallas_call(
        score_kernel,
        out_shape=(
            jax.ShapeDtypeStruct((D, NEG), F32),
            jax.ShapeDtypeStruct((2, D, TRIP), BF),
            jax.ShapeDtypeStruct((224, TRIP), BF),
            jax.ShapeDtypeStruct((448, 128), F32),
            jax.ShapeDtypeStruct((2, TRIP), jnp.int32),
        ),
        in_specs=[VM] * 6 + [ANY] * 2,
        out_specs=(VM,) * 5,
        scratch_shapes=[
            v((NB, NREL), F32), v((D, ENT), BF), v((224, 1024), BF), v((1024, TRIP), BF), v((224, TRIP), F32),
            v((NB, TRIP), F32), v((D, TRIP), F32), v((D, TRIP), BF), v((TRIP, D), BF), v((D, TRIP), F32),
            v((2, 4, 4, D, NEG), BF), v((2, 4, 4, D, NEG), BF), v((4, 4, D, NEG), BF),
            v((3, 4, 208, NEG), BF), v((3, 4, 192, NEG), BF), v((4, 208, NEG), BF), v((4, 192, NEG), BF),
            v((3, D, NEG), BF), v((D, 512), BF),
            sem((48,)), sem((48,)), sem((2,)),
        ],
        compiler_params=pltpu.CompilerParams(collective_id=0, has_side_effects=True, vmem_limit_bytes=56 * 2**20),
        cost_estimate=pl.CostEstimate(flops=10**11, bytes_accessed=10**7, transcendentals=4 * 10**6),
        name="score",
    )(head, tail, rel, owners, negr, basest, coeft, entt)


def pack_kernel(pos, orow, grads, out, gn, low):
    step = pl.program_id(0)

    @pl.when(step == 0)
    def _():
        for h in range(2):
            at = h * TRIP
            low[:, at : at + TRIP] = spread(pos[h : h + 1] & 255, 256)
            r = orow[h : h + 1].astype(jnp.int32)
            two = lax.broadcasted_iota(jnp.int32, (112, TRIP), 0)
            extra = jnp.where(two == 0, lax.shift_right_logical(r, 6), jnp.where(two == 1, r & 63, 0))
            g = jnp.concatenate([grads[h], extra.astype(F32).astype(BF)], axis=0)
            gn[at : at + TRIP, :] = g.T

    tot = None
    for h in range(2):
        at = h * TRIP
        one = low[:, at : at + TRIP] * equals(lax.shift_right_logical(pos[h : h + 1], 8), step)
        d = dot(one, gn[at : at + TRIP])
        tot = d if tot is None else tot + d
    out[...] = tot.astype(BF)


def pack(pos, orow, grads):
    whole = lambda *s: pl.BlockSpec(s, lambda i: (0,) * len(s))
    return pl.pallas_call(
        pack_kernel,
        grid=(16,),
        out_shape=jax.ShapeDtypeStruct((4096, 512), BF),
        in_specs=[whole(2, TRIP), whole(2, TRIP), whole(2, D, TRIP)],
        out_specs=pl.BlockSpec((256, 512), lambda i: (i, 0)),
        scratch_shapes=[pltpu.VMEM((2 * TRIP, 512), BF), pltpu.VMEM((256, 2 * TRIP), BF)],
        compiler_params=pltpu.CompilerParams(vmem_limit_bytes=40 * 2**20),
        cost_estimate=pl.CostEstimate(flops=9 * 10**9, bytes_accessed=6 * 10**6, transcendentals=0),
        name="pack",
    )(pos, orow, grads)


WIDE = 4096 + 2 * NEG


def place_kernel(recv, own_neg, negr, out, rt, low, ids):
    step = pl.program_id(0)

    @pl.when(step == 0)
    def _():
        for q in range(8):
            at = q * 512
            rt[:, at : at + 512] = recv[at : at + 512, :].T
            a = rt[400:416, at : at + 512].astype(F32)
            ids[:, at : at + 512] = (a[0:1] * 64.0 + a[1:2]).astype(jnp.int32)
        n = own_neg[...]
        first = n.astype(BF)
        rt[0:D, 4096 : 4096 + NEG] = first
        rt[0:D, 4096 + NEG : WIDE] = (n - first.astype(F32)).astype(BF)
        ids[:, 4096 : 4096 + NEG] = negr[...]
        ids[:, 4096 + NEG : WIDE] = negr[...]
        low[...] = spread(ids[...] & 255, 256)

    one = low[...] * equals(lax.shift_right_logical(ids[...], 8), step)
    out[...] = dot(rt[0:D, :], one, 1, 1)


def place(recv, own_neg, negr):
    whole = lambda *s: pl.BlockSpec(s, lambda i: (0,) * len(s))
    return pl.pallas_call(
        place_kernel,
        grid=(16,),
        out_shape=jax.ShapeDtypeStruct((D, ENT), F32),
        in_specs=[whole(4096, 512), whole(D, NEG), whole(1, NEG)],
        out_specs=pl.BlockSpec((D, 256), lambda i: (0, i)),
        scratch_shapes=[pltpu.VMEM((512, WIDE), BF), pltpu.VMEM((256, WIDE), BF), pltpu.VMEM((1, WIDE), jnp.int32)],
        compiler_params=pltpu.CompilerParams(vmem_limit_bytes=40 * 2**20),
        cost_estimate=pl.CostEstimate(flops=14 * 10**9, bytes_accessed=11 * 10**6, transcendentals=0),
        name="place",
    )(recv, own_neg, negr)


RANGE = 1920


def reduce_kernel(
    rows, rel, bpart, out,
    gr, gi, gb, acc, rsb, r2a, r2b, s3a, s3b, r3, ss, rs, loc,
):
    z, k = lax.axis_index("grp"), lax.axis_index("dev")
    x, y, c = k // 8, lax.rem(k // 2, 4), lax.rem(k, 2)
    own = z * 2 + c

    def dev(dx, dy, dz, dc):
        return (lax.rem(z + dz, 4), (lax.rem(x + dx, 4) * 4 + lax.rem(y + dy, 4)) * 2 + lax.rem(c + dc, 2))

    XP = [dev(d, 0, 0, 0) for d in (1, 2, 3)]
    YP = [dev(0, d, 0, 0) for d in (1, 2, 3)]
    ZP = [dev(0, 0, d, 0) for d in (1, 2, 3)]
    ZC = [dev(0, 0, d, 1) for d in (1, 2, 3)]
    CP = dev(0, 0, 0, 1)
    bar = pltpu.get_barrier_semaphore()
    for p in XP + YP + ZP + ZC + [CP]:
        pl.semaphore_signal(bar, inc=1, device_id=p, device_id_type=MESH)
    keep = [
        pltpu.make_async_copy(rows, gr.at[own], loc.at[0]),
        pltpu.make_async_copy(rel, gi.at[own], loc.at[1]),
        pltpu.make_async_copy(bpart.at[pl.ds(pl.multiple_of(own * 56, 8), 56)], gb.at[own], loc.at[2]),
    ]
    for cp in keep:
        cp.start()
    count = [0]
    sent = []

    def send(src, dst, p):
        i = count[0]
        count[0] += 1
        cp = pltpu.make_async_remote_copy(
            src_ref=src, dst_ref=dst, send_sem=ss.at[i], recv_sem=rs.at[i], device_id=p, device_id_type=MESH
        )
        cp.start()
        sent.append(cp)
        return cp

    for cp in keep:
        cp.wait()
    pl.semaphore_wait(bar, 13)
    first = [
        [send(rel, gi.at[own], ZP[d]), send(rows, gr.at[own], ZP[d])] for d in (0, 2, 1)
    ]
    near = [send(rel, gi.at[own], CP), send(rows, gr.at[own], CP)]
    pieces = []

    def piece(dz, dc, p):
        r = lax.rem(z + dz, 4) * 2 + lax.rem(c + dc, 2)
        pieces.append(send(bpart.at[pl.ds(pl.multiple_of(r * 56, 8), 56)], gb.at[own], p))

    piece(0, 1, CP)
    for d in (1, 2, 3):
        piece(d, 0, ZP[d - 1])
        piece(d, 1, ZC[d - 1])

    def add(j, start):
        ids = gi[j] - own * RANGE
        low = spread(ids & 255, 256)
        high = lax.shift_right_arithmetic(ids, 8)
        r = gr[j]
        for t in range(8):
            p = dot(r * equals(high, t), low, 1, 1)
            p = p[0:104] + p[LOROW : LOROW + 104]
            if start:
                acc[t] = p
            else:
                acc[t] += p

    add(own, True)
    for cp in near:
        cp.wait_recv()
    add(z * 2 + 1 - c, False)
    more = []
    for i, d in enumerate((1, 3, 2)):
        src = lax.rem(z - d + 4, 4) * 2
        for cp in first[i]:
            cp.wait_recv()
        more = [send(gi.at[src + c], gi.at[src + c], CP), send(gr.at[src + c], gr.at[src + c], CP)]
        add(src + c, False)
        for cp in more:
            cp.wait_recv()
        add(src + 1 - c, False)
    for cp in pieces:
        cp.wait_recv()
    tot = gb[0]
    for j in range(1, 8):
        tot += gb[j]
    for q in range(16):
        if q == 15:
            rsb[3, 3] = jnp.zeros((104, 128), F32)
            rsb[3, 3, 0:56] = tot
        else:
            rsb[q // 4, q % 4] = acc[q // 2, :, (q % 2) * 128 : (q % 2) * 128 + 128]
    A, B = pl.ds(0, 56), pl.ds(56, 48)
    a4, b4 = [], []
    for d in (2, 1, 3):
        yy, xx = lax.rem(y + d, 4), lax.rem(x + d, 4)
        a4.append(send(rsb.at[yy, :, A], r2a.at[d - 1], YP[d - 1]))
        b4.append(send(rsb.at[:, xx, B], r2b.at[d - 1], XP[d - 1]))
    for cp in a4:
        cp.wait_recv()
    t4 = rsb[y, :, 0:56, :]
    for d in range(3):
        t4 += r2a[d]
    s3a[...] = t4
    a5 = [send(s3a.at[lax.rem(x + d, 4)], r3.at[d - 1, A], XP[d - 1]) for d in (2, 1, 3)]
    for cp in b4:
        cp.wait_recv()
    t4 = rsb[:, x, 56:104, :]
    for d in range(3):
        t4 += r2b[d]
    s3b[...] = t4
    b5 = [send(s3b.at[lax.rem(y + d, 4)], r3.at[d - 1, B], YP[d - 1]) for d in (2, 1, 3)]
    for cp in a5:
        cp.wait_recv()
    ta = s3a[x]
    for d in range(3):
        ta += r3[d, 0:56]
    for cp in b5:
        cp.wait_recv()
    tb = s3b[y]
    for d in range(3):
        tb += r3[d, 56:104]
    done = jnp.concatenate([ta, tb, jnp.zeros((8, 128), F32)], axis=0).astype(BF)
    out[c, z, y, x] = done
    S = (pl.ds(0, 48), pl.ds(48, 32), pl.ds(80, 32))
    w0, w1, w2 = (out.at[c, z, y, x, s] for s in S)
    st1 = [[send(w, w, p) for p in P] for w, P in ((w0, XP), (w1, YP), (w2, ZP))]
    w0, w1, w2 = out.at[c, z, y, :, S[0]], out.at[c, z, :, x, S[1]], out.at[c, :, y, x, S[2]]
    st2 = []
    for i, (w, P) in enumerate(((w0, YP), (w1, ZP), (w2, XP))):
        for cp in st1[i]:
            cp.wait_recv()
        st2.append([send(w, w, p) for p in P])
    w0, w1, w2 = out.at[c, z, :, :, S[0]], out.at[c, :, :, x, S[1]], out.at[c, :, y, :, S[2]]
    st3, last = [], []
    for i, (w, P) in enumerate(((w0, ZP), (w1, XP), (w2, YP))):
        for cp in st2[i]:
            cp.wait_recv()
        st3.append([send(w, w, P[d]) for d in (1, 0, 2)])
        last.append(send(w, w, CP))
    for i in range(3):
        for j, d in ((1, 1), (2, 3), (0, 2)):
            st3[i][j].wait_recv()
            if i == 0:
                w = out.at[c, lax.rem(z - d + 4, 4), :, :, S[0]]
            elif i == 1:
                w = out.at[c, :, :, lax.rem(x - d + 4, 4), S[1]]
            else:
                w = out.at[c, :, lax.rem(y - d + 4, 4), :, S[2]]
            last.append(send(w, w, CP))
    for cp in last:
        cp.wait_recv()
    for cp in sent:
        cp.wait_send()


def reduce_all(rows, rel, bpart):
    sem = pltpu.SemaphoreType.DMA
    v = pltpu.VMEM
    return pl.pallas_call(
        reduce_kernel,
        out_shape=jax.ShapeDtypeStruct((2, 4, 4, 4, 112, 128), BF),
        in_specs=[VM] * 3,
        out_specs=VM,
        scratch_shapes=[
            v((8, 224, TRIP), BF), v((8, 1, TRIP), jnp.int32), v((8, 56, 128), F32), v((8, 104, 256), F32),
            v((4, 4, 104, 128), F32), v((3, 4, 56, 128), F32), v((3, 4, 48, 128), F32),
            v((4, 56, 128), F32), v((4, 48, 128), F32), v((3, 104, 128), F32),
            sem((80,)), sem((80,)), sem((3,)),
        ],
        compiler_params=pltpu.CompilerParams(collective_id=1, has_side_effects=True, vmem_limit_bytes=40 * 2**20),
        cost_estimate=pl.CostEstimate(flops=8 * 10**10, bytes_accessed=10**7, transcendentals=0),
        name="reduce",
    )(rows, rel, bpart)


def unpack_kernel(tiles, coef_out, bases_out):
    r = pl.program_id(0)
    z, c = r // 2, r % 2
    for q in range(15):
        coef_out[:, q * 128 : (q + 1) * 128] = tiles[c, z, q // 4, q % 4, 0:NB].astype(F32)

    @pl.when(r == 0)
    def _():
        for j in range(8):
            n = min(56, D - 56 * j)
            if n > 0:
                bases_out[56 * j : 56 * j + n, :] = tiles[j % 2, j // 2, 3, 3, 0:n, 0:NB].astype(F32)


def unpack(tiles):
    return pl.pallas_call(
        unpack_kernel,
        grid=(8,),
        out_shape=(jax.ShapeDtypeStruct((NB, NREL), F32), jax.ShapeDtypeStruct((D, NB), F32)),
        in_specs=[pl.BlockSpec((2, 4, 4, 4, 112, 128), lambda i: (0,) * 6)],
        out_specs=(pl.BlockSpec((NB, RANGE), lambda i: (0, i)), pl.BlockSpec((D, NB), lambda i: (0, 0))),
        compiler_params=pltpu.CompilerParams(vmem_limit_bytes=40 * 2**20),
        name="unpack",
    )(tiles)


def per_device(head_emb, tail_emb, relation, owners, owner_rows, entities, neg_rows, coef, bases):
    rel = relation.reshape(1, TRIP)
    own_neg, grads, rows, bases_part, pos = score(
        head_emb.T, tail_emb.T, rel, owners.T, neg_rows, bases.T, coef.T, entities.T
    )
    packed = pack(pos, owner_rows.T, grads)
    recv = lax.all_to_all(packed, ("grp", "dev"), split_axis=0, concat_axis=0, tiled=True)
    tiles = reduce_all(rows, rel, bases_part)
    coef_grad, bases_grad = unpack(tiles)
    ent_grad = place(recv, own_neg, neg_rows)
    return ent_grad.T, coef_grad.T, bases_grad.T


def solution(mesh):
    rows = P(("grp", "dev"), None)
    return jax.shard_map(
        per_device,
        mesh=mesh,
        in_specs=(rows, rows, P(("grp", "dev")), rows, rows, rows, P(None, ("grp", "dev")), P(), P()),
        out_specs=(rows, P(), P()),
        check_vma=False,
    )
```

time: 430 us -> 218 us (0.51); the launches traced: 422 us -> 217 us
  waiting for transfers between devices: 207 us -> 0.01 us
  Pallas kernels: 0 us -> 203 us
  local copies, waits for them, and re-layouts: 93.8 us -> 4.15 us
  other arithmetic: 57.2 us -> 0 us
  matrix products: 32.9 us -> 0 us
  between operations: 14.2 us -> 0.75 us
  starting transfers between devices: 17.1 us -> 8.68 us
    pallas_call x0 -> x5, Pallas kernels: none -> 203 us  [the longest x1 108 us: reduce_all(): pl.pallas_call(reduce_kernel, out_shape=jax.ShapeDtypeStruct((2, 4, 4, 4,...]
    psum x1 -> x0, waiting for transfers between devices: 101 us -> none  [per_device(): coef_grad, bases_grad = lax.psum((coef_local, bases_local), ('grp', 'dev'))]
    unnamed x4 -> x0, waiting for transfers between devices: 74.8 us -> none
    scatter-add x3 -> x0, other arithmetic: 48.2 us -> none  [the longest x1 33.3 us: per_device(): ent_grad = ent_grad.at[recv_index].add(recv_rows.astype(jnp.float32))]
    unnamed x39 -> x18, local copies, waits for them, and re-layouts: 42.6 us -> 4.15 us
    dot_general x6 -> x0, matrix products: 32.9 us -> none  [the longest x1 9.87 us: per_device(): lax.dot_general(probs_part, head_rel, (((0,), (0,)), ((), ())), preferred...]
    all_gather x1 -> x0, waiting for transfers between devices: 31.3 us -> none  [per_device(): group_negs = lax.all_gather(local_negs, 'dev', axis=1, tiled=True)]
    scatter x2 -> x0, local copies, waits for them, and re-layouts: 20.9 us -> none  [the longest x1 12.8 us: per_device(): jnp.zeros((all_devices * capacity, columns), jnp.bfloat16).at[position]]
  transfers between devices with their start and end apart: 5 -> 1, of which waited for: 3 -> 0; matrix products, arithmetic and copies ran while one was open for 23% -> 0% of each run, Pallas kernels for 0% -> 52%
where the time goes in v1:
time: 218 us; the launch traced here: 217 us
  Pallas kernels  203 us (93%)
  starting transfers between devices  8.68 us (4%)
  local copies, waits for them, and re-layouts  4.15 us (2%)
    pallas_call x1, Pallas kernels, reduce_all(): pl.pallas_call(reduce_kernel, out_shape=jax.ShapeDtypeStruct((2, 4, 4, 4,...  108 us
    pallas_call x1, Pallas kernels, score(): pl.pallas_call(score_kernel, out_shape=(jax.ShapeDtypeStruct((D, NEG), F3...  55.2 us
    pallas_call x1, Pallas kernels, place(): pl.pallas_call(place_kernel, grid=(16,), out_shape=jax.ShapeDtypeStruct((...  22.9 us
    pallas_call x1, Pallas kernels, pack(): pl.pallas_call(pack_kernel, grid=(16,), out_shape=jax.ShapeDtypeStruct((4...  12.4 us
    all_to_all x1, starting transfers between devices, per_device(): lax.all_to_all(packed, ('grp', 'dev'), split_axis=0, concat_axis=0, tiled...  8.68 us
  transfers between devices with their start and end apart: 1, of which 0 were waited for; matrix products, arithmetic and copies ran while one was open for 0% of the time, Pallas kernels for 52%

profile of v1, /device:TPU:1, one launch (start us, length us, event | category | flops | bytes accessed | tf_op | source)
XLA Modules:
  0.0 216.6 jit_solution(13353498772505912725)
XLA Ops:
  0.6 0.0 copy-start.1
  0.6 55.2 %score.1 = (f32[400,128]{1,0:T(8,128)}, bf16[2,400,1024]{2,1,0:T(8,128)(2,1)}, bf16[224,1024]{1,0:T(8,128)(2,1)}, f32[448,128]{1,0:T(8,128)}, s32[2,1024]{1,0:T(2,128)}) custom-call(bf16[400,1024]{1,0:T(8,128)(2,1)} %bitcast.20, bf16[400,1024]{1,0:T(8,128)(2,1)} %bitcast.21, s32[1,1024]{1,0:T(1,128)} %bitcast.15, s32[2,1024]{1,0:T(2,128)} %bitcast.24, ...), custom_call_target="tpu_custom_call" | custom-call | flops 99999997952 | bytes 10000000 | tf_op jit(solution)/shard_map/score/pallas_call | solution.py:245
  55.8 0.0 copy-done.1
  55.9 0.0 copy-start.4
  55.9 1.4 copy-done.4
  57.3 0.0 copy-start.6
  57.3 0.7 copy-done.6
  58.0 12.4 %pack.1 = bf16[4096,512]{1,0:T(8,128)(2,1)S(1)} custom-call(s32[2,1024]{1,0:T(2,128)S(1)} %copy-done.6, s32[2,1024]{1,0:T(2,128)S(1)} %bitcast.14, bf16[2,400,1024]{2,1,0:T(8,128)(2,1)S(1)} %copy-done.4), custom_call_target="tpu_custom_call" | custom-call | flops 8999999488 | bytes 6000000 | tf_op jit(solution)/shard_map/pack/pallas_call | solution.py:295
  70.4 0.0 copy-start
  70.4 2.0 copy-done
  72.4 0.0 copy-start.2
  72.4 0.0 copy-start.7
  72.4 8.7 %all-to-all-start = ((bf16[128,32,512]{2,1,0:T(8,128)(2,1)}), bf16[128,32,512]{2,1,0:T(8,128)(2,1)}, u32[]{:S(2)}, u32[]{:S(2)}) async-start(bf16[128,32,512]{2,1,0:T(8,128)(2,1)} %bitcast.13), calls=%async_computation | async-start | bytes 8388608 | tf_op jit(solution)/shard_map/all_to_all | solution.py:562
  81.1 0.0 copy-done.2
  81.1 0.0 copy-done.7
  81.2 0.0 copy-done.8
  81.2 0.0 copy-start.3
  81.2 0.0 copy-start.5
  81.2 108.5 %reduce.1.tiles = bf16[2,4,4,4,112,128]{5,4,3,2,1,0:T(8,128)(2,1)S(1)} custom-call(bf16[224,1024]{1,0:T(8,128)(2,1)S(1)} %copy-done.7, s32[1,1024]{1,0:T(1,128)S(1)} %bitcast.16, f32[448,128]{1,0:T(8,128)S(1)} %copy-done.8), custom_call_target="tpu_custom_call" | custom-call | flops 80000000000 | bytes 10000000 | tf_op jit(solution)/shard_map/reduce/pallas_call | solution.py:513
  189.7 4.0 %unpack.1 = (f32[100,14824]{1,0:T(8,128)}, f32[400,100]{1,0:T(8,128)}) custom-call(bf16[2,4,4,4,112,128]{5,4,3,2,1,0:T(8,128)(2,1)S(1)} %reduce.1.tiles), custom_call_target="tpu_custom_call" | custom-call | tf_op jit(solution)/shard_map/unpack/pallas_call | solution.py:545
  193.7 0.0 all-to-all-done
  193.7 0.0 copy-done.3
  193.7 0.0 copy-done.5
  193.7 22.9 %place.1 = f32[400,4096]{1,0:T(8,128)} custom-call(bf16[4096,512]{1,0:T(8,128)(2,1)} %bitcast.9.recv, f32[400,128]{1,0:T(8,128)S(1)} %copy-done.5, s32[1,128]{1,0:T(1,128)S(1)} %copy-done.3), custom_call_target="tpu_custom_call" | custom-call | flops 14000000000 | bytes 11000000 | tf_op jit(solution)/shard_map/place/pallas_call | solution.py:335
  (1 shorter events, 0.0 us)
Async XLA Ops:
  0.6 55.2 %copy-start.1 = (s32[1024,2]{0,1:T(2,128)S(1)}, s32[1024,2]{0,1:T(2,128)}, u32[]{:S(2)}) copy-start(s32[1024,2]{0,1:T(2,128)} %param.13) | copy-start | bytes 24580
  55.9 1.4 copy-start.4
  57.3 0.7 copy-start.6
  70.4 2.0 copy-start
  72.4 8.7 %copy-start.2 = (s32[1024]{0:T(1024)S(1)}, s32[1024]{0:T(1024)}, u32[]{:S(2)}) copy-start(s32[1024]{0:T(1024)} %param.11) | copy-start | bytes 12292
  72.4 8.7 %copy-start.7 = (bf16[224,1024]{1,0:T(8,128)(2,1)S(1)}, bf16[224,1024]{1,0:T(8,128)(2,1)}, u32[]{:S(2)}) copy-start(bf16[224,1024]{1,0:T(8,128)(2,1)} %get-tuple-element.13.rows) | copy-start | bytes 1376260
  72.4 8.7 %copy-start.8 = (f32[448,128]{1,0:T(8,128)S(1)}, f32[448,128]{1,0:T(8,128)}, u32[]{:S(2)}) copy-start(f32[448,128]{1,0:T(8,128)} %get-tuple-element.14.bpart) | copy-start | bytes 688132
  72.4 121.3 %all-to-all-start = ((bf16[128,32,512]{2,1,0:T(8,128)(2,1)}), bf16[128,32,512]{2,1,0:T(8,128)(2,1)}, u32[]{:S(2)}, u32[]{:S(2)}) async-start(bf16[128,32,512]{2,1,0:T(8,128)(2,1)} %bitcast.13), calls=%async_computation | async-start | bytes 8388608 | tf_op jit(solution)/shard_map/all_to_all | solution.py:562
  81.2 112.6 %copy-start.3 = (s32[1,128]{1,0:T(1,128)S(1)}, s32[1,128]{1,0:T(1,128)}, u32[]{:S(2)}) copy-start(s32[1,128]{1,0:T(1,128)} %negr.3) | copy-start | bytes 1540
  81.2 112.6 %copy-start.5 = (f32[400,128]{1,0:T(8,128)S(1)}, f32[400,128]{1,0:T(8,128)}, u32[]{:S(2)}) copy-start(f32[400,128]{1,0:T(8,128)} %get-tuple-element.12.own_neg) | copy-start | bytes 614404

commit v2 on v1

--- a/solution.py
+++ b/solution.py
@@ -147,7 +147,13 @@
             onef = one.astype(F32)
             rank = jnp.sum((dot(one, tri) + before) * onef, axis=0, keepdims=True)
             before = before + jnp.sum(onef, axis=1, keepdims=True)
-            pos[h : h + 1, b * 256 : (b + 1) * 256] = o * 32 + rank.astype(jnp.int32)
+            chip = lax.shift_right_logical(o, 1)
+            pos[h : h + 1, b * 256 : (b + 1) * 256] = (
+                lax.shift_right_logical(chip, 1) * 128
+                + lax.rem((chip & 1) + c, 2) * 64
+                + lax.rem((o & 1) + y, 2) * 32
+                + rank.astype(jnp.int32)
+            )
 
     for j, d in ((1, 1), (2, 3), (0, 2)):
         a2[j].wait_recv()
@@ -267,57 +273,19 @@
     )(head, tail, rel, owners, negr, basest, coeft, entt)
 
 
-def pack_kernel(pos, orow, grads, out, gn, low):
+WIDE = 4096 + 2 * NEG
+HALF = 208
+
+
+def place_kernel(recv, own_neg, negr, out, rt, low, ids):
     step = pl.program_id(0)
 
     @pl.when(step == 0)
     def _():
-        for h in range(2):
-            at = h * TRIP
-            low[:, at : at + TRIP] = spread(pos[h : h + 1] & 255, 256)
-            r = orow[h : h + 1].astype(jnp.int32)
-            two = lax.broadcasted_iota(jnp.int32, (112, TRIP), 0)
-            extra = jnp.where(two == 0, lax.shift_right_logical(r, 6), jnp.where(two == 1, r & 63, 0))
-            g = jnp.concatenate([grads[h], extra.astype(F32).astype(BF)], axis=0)
-            gn[at : at + TRIP, :] = g.T
-
-    tot = None
-    for h in range(2):
-        at = h * TRIP
-        one = low[:, at : at + TRIP] * equals(lax.shift_right_logical(pos[h : h + 1], 8), step)
-        d = dot(one, gn[at : at + TRIP])
-        tot = d if tot is None else tot + d
-    out[...] = tot.astype(BF)
-
-
-def pack(pos, orow, grads):
-    whole = lambda *s: pl.BlockSpec(s, lambda i: (0,) * len(s))
-    return pl.pallas_call(
-        pack_kernel,
-        grid=(16,),
-        out_shape=jax.ShapeDtypeStruct((4096, 512), BF),
-        in_specs=[whole(2, TRIP), whole(2, TRIP), whole(2, D, TRIP)],
-        out_specs=pl.BlockSpec((256, 512), lambda i: (i, 0)),
-        scratch_shapes=[pltpu.VMEM((2 * TRIP, 512), BF), pltpu.VMEM((256, 2 * TRIP), BF)],
-        compiler_params=pltpu.CompilerParams(vmem_limit_bytes=40 * 2**20),
-        cost_estimate=pl.CostEstimate(flops=9 * 10**9, bytes_accessed=6 * 10**6, transcendentals=0),
-        name="pack",
-    )(pos, orow, grads)
-
-
-WIDE = 4096 + 2 * NEG
-
-
-def place_kernel(recv, own_neg, negr, out, rt, low, ids):
-    step = pl.program_id(0)
-
-    @pl.when(step == 0)
-    def _():
-        for q in range(8):
-            at = q * 512
-            rt[:, at : at + 512] = recv[at : at + 512, :].T
-            a = rt[400:416, at : at + 512].astype(F32)
-            ids[:, at : at + 512] = (a[0:1] * 64.0 + a[1:2]).astype(jnp.int32)
+        rt[0:HALF, 0:4096] = recv[0]
+        rt[HALF:D, 0:4096] = recv[1, 0 : D - HALF]
+        a = recv[1, D - HALF : HALF].astype(F32)
+        ids[:, 0:4096] = (a[0:1] * 64.0 + a[1:2]).astype(jnp.int32)
         n = own_neg[...]
         first = n.astype(BF)
         rt[0:D, 4096 : 4096 + NEG] = first
@@ -336,9 +304,9 @@
         place_kernel,
         grid=(16,),
         out_shape=jax.ShapeDtypeStruct((D, ENT), F32),
-        in_specs=[whole(4096, 512), whole(D, NEG), whole(1, NEG)],
+        in_specs=[whole(2, HALF, 4096), whole(D, NEG), whole(1, NEG)],
         out_specs=pl.BlockSpec((D, 256), lambda i: (0, i)),
-        scratch_shapes=[pltpu.VMEM((512, WIDE), BF), pltpu.VMEM((256, WIDE), BF), pltpu.VMEM((1, WIDE), jnp.int32)],
+        scratch_shapes=[pltpu.VMEM((D, WIDE), BF), pltpu.VMEM((256, WIDE), BF), pltpu.VMEM((1, WIDE), jnp.int32)],
         compiler_params=pltpu.CompilerParams(vmem_limit_bytes=40 * 2**20),
         cost_estimate=pl.CostEstimate(flops=14 * 10**9, bytes_accessed=11 * 10**6, transcendentals=0),
         name="place",
@@ -348,9 +316,10 @@
 RANGE = 1920
 
 
-def reduce_kernel(
-    rows, rel, bpart, out,
-    gr, gi, gb, acc, rsb, r2a, r2b, s3a, s3b, r3, ss, rs, loc,
+def exchange_kernel(
+    rows, rel, bpart, pos, orow, grads, out, recv,
+    gr, gi, gb, acc, rsb, r2a, r2b, s3a, s3b, r3,
+    gx, low, pk, pb, w, v, u, xx, px, ss, rs, loc,
 ):
     z, k = lax.axis_index("grp"), lax.axis_index("dev")
     x, y, c = k // 8, lax.rem(k // 2, 4), lax.rem(k, 2)
@@ -364,40 +333,57 @@
     ZP = [dev(0, 0, d, 0) for d in (1, 2, 3)]
     ZC = [dev(0, 0, d, 1) for d in (1, 2, 3)]
     CP = dev(0, 0, 0, 1)
+    xs = [lax.rem(x + d, 4) for d in range(4)]
+    ys = [lax.rem(y + d, 4) for d in range(4)]
+    zs = [lax.rem(z + d, 4) for d in range(4)]
     bar = pltpu.get_barrier_semaphore()
     for p in XP + YP + ZP + ZC + [CP]:
         pl.semaphore_signal(bar, inc=1, device_id=p, device_id_type=MESH)
-    keep = [
-        pltpu.make_async_copy(rows, gr.at[own], loc.at[0]),
-        pltpu.make_async_copy(rel, gi.at[own], loc.at[1]),
-        pltpu.make_async_copy(bpart.at[pl.ds(pl.multiple_of(own * 56, 8), 56)], gb.at[own], loc.at[2]),
+    local = []
+
+    def keep(src, dst):
+        cp = pltpu.make_async_copy(src, dst, loc.at[len(local)])
+        cp.start()
+        local.append(cp)
+        return cp
+
+    kept = [
+        keep(rows, gr.at[own]),
+        keep(rel, gi.at[own]),
+        keep(bpart.at[pl.ds(pl.multiple_of(own * 56, 8), 56)], gb.at[own]),
     ]
-    for cp in keep:
-        cp.start()
-    count = [0]
+    count = [16]
     sent = []
 
-    def send(src, dst, p):
-        i = count[0]
-        count[0] += 1
-        cp = pltpu.make_async_remote_copy(
+    def remote(src, dst, i, p):
+        return pltpu.make_async_remote_copy(
             src_ref=src, dst_ref=dst, send_sem=ss.at[i], recv_sem=rs.at[i], device_id=p, device_id_type=MESH
         )
+
+    def send(src, dst, p):
+        cp = remote(src, dst, count[0], p)
+        count[0] += 1
         cp.start()
         sent.append(cp)
         return cp
 
-    for cp in keep:
+    for h in range(2):
+        at = h * TRIP
+        low[:, at : at + TRIP] = spread(pos[h : h + 1] & 255, 256)
+        r = orow[h : h + 1]
+        two = lax.broadcasted_iota(jnp.int32, (16, TRIP), 0)
+        extra = jnp.where(two == 0, lax.shift_right_logical(r, 6), jnp.where(two == 1, r & 63, 0))
+        gx[0:D, at : at + TRIP] = grads[h]
+        gx[D : D + 16, at : at + TRIP] = extra.astype(F32).astype(BF)
+    for cp in kept:
         cp.wait()
     pl.semaphore_wait(bar, 13)
-    first = [
-        [send(rel, gi.at[own], ZP[d]), send(rows, gr.at[own], ZP[d])] for d in (0, 2, 1)
-    ]
+    first = [[send(rel, gi.at[own], ZP[d]), send(rows, gr.at[own], ZP[d])] for d in (0, 2, 1)]
     near = [send(rel, gi.at[own], CP), send(rows, gr.at[own], CP)]
     pieces = []
 
     def piece(dz, dc, p):
-        r = lax.rem(z + dz, 4) * 2 + lax.rem(c + dc, 2)
+        r = zs[dz] * 2 + lax.rem(c + dc, 2)
         pieces.append(send(bpart.at[pl.ds(pl.multiple_of(r * 56, 8), 56)], gb.at[own], p))
 
     piece(0, 1, CP)
@@ -405,13 +391,76 @@
         piece(d, 0, ZP[d - 1])
         piece(d, 1, ZC[d - 1])
 
+    S = (pl.ds(0, 80), pl.ds(80, 64), pl.ds(144, 64))
+    high = [lax.shift_right_logical(pos[h : h + 1], 8) for h in range(2)]
+    lane = lax.broadcasted_iota(jnp.int32, (HALF, 128), 1)
+    side = (lane // 64) == c
+    st1 = [[], [], []]
+
+    def swap(s):
+        return remote(pk.at[1 - c, s], pb.at[s], s, CP)
+
+    for gp in range(4):
+        zz = zs[(gp + 1) % 4]
+
+        def fill(j, carry):
+            s = zz * 4 + j
+            tot = None
+            for h in range(2):
+                at = h * TRIP
+                one = low[:, at : at + TRIP] * equals(high[h], s)
+                d = dot(gx[:, at : at + TRIP], one, 1, 1)
+                tot = d if tot is None else tot + d
+            pk[0, s] = tot[0:HALF].astype(BF)
+            pk[1, s] = tot[HALF : 2 * HALF].astype(BF)
+            swap(s).start()
+            return carry
+
+        def join(j, carry):
+            s = zz * 4 + j
+            swap(s).wait()
+            for q in range(2):
+                a = pk[c, s, :, q * 128 : (q + 1) * 128]
+                b = pb[s, :, q * 128 : (q + 1) * 128]
+                w[zz, j, 2 * q] = jnp.where(side, a, b)
+                w[zz, j, 2 * q + 1] = jnp.where(side, b, a)
+            return carry
+
+        lax.fori_loop(0, 4, fill, 0)
+        lax.fori_loop(0, 4, join, 0)
+        for d in (1, 3, 2):
+            st1[0].append(send(w.at[zz, xs[d], :, S[0]], v.at[zz, x, :, S[0]], XP[d - 1]))
+            st1[1].append(send(w.at[zz, :, ys[d], S[1]], v.at[zz, :, y, S[1]], YP[d - 1]))
+        if gp < 3:
+            st1[2].append(send(w.at[zz, :, :, S[2]], v.at[z, :, :, S[2]], ZP[gp]))
+    st1[0].append(keep(w.at[:, x, :, S[0]], v.at[:, x, :, S[0]]))
+    st1[1].append(keep(w.at[:, :, y, S[1]], v.at[:, :, y, S[1]]))
+    st1[2].append(keep(w.at[z, :, :, S[2]], v.at[z, :, :, S[2]]))
+
+    def arrived(cps):
+        for cp in cps[:-1]:
+            cp.wait_recv()
+        cps[-1].wait()
+
+    def along_x(a, b, s):
+        cps = [send(a.at[:, xs[d], :, s], b.at[:, x, :, s], XP[d - 1]) for d in (1, 3, 2)]
+        return cps + [keep(a.at[:, x, :, s], b.at[:, x, :, s])]
+
+    def along_y(a, b, s):
+        cps = [send(a.at[:, :, ys[d], s], b.at[:, :, y, s], YP[d - 1]) for d in (1, 3, 2)]
+        return cps + [keep(a.at[:, :, y, s], b.at[:, :, y, s])]
+
+    def along_z(a, b, s):
+        cps = [send(a.at[zs[d], :, :, s], b.at[z, :, :, s], ZP[d - 1]) for d in (1, 3, 2)]
+        return cps + [keep(a.at[z, :, :, s], b.at[z, :, :, s])]
+
     def add(j, start):
         ids = gi[j] - own * RANGE
-        low = spread(ids & 255, 256)
-        high = lax.shift_right_arithmetic(ids, 8)
+        lo = spread(ids & 255, 256)
+        hi = lax.shift_right_arithmetic(ids, 8)
         r = gr[j]
         for t in range(8):
-            p = dot(r * equals(high, t), low, 1, 1)
+            p = dot(r * equals(hi, t), lo, 1, 1)
             p = p[0:104] + p[LOROW : LOROW + 104]
             if start:
                 acc[t] = p
@@ -422,16 +471,21 @@
     for cp in near:
         cp.wait_recv()
     add(z * 2 + 1 - c, False)
-    more = []
+
+    st2 = []
+    for i, go in enumerate((along_y, along_z, along_x)):
+        arrived(st1[i])
+        st2.append(go(v, u, S[i]))
+
     for i, d in enumerate((1, 3, 2)):
-        src = lax.rem(z - d + 4, 4) * 2
+        from_z = lax.rem(z - d + 4, 4) * 2
         for cp in first[i]:
             cp.wait_recv()
-        more = [send(gi.at[src + c], gi.at[src + c], CP), send(gr.at[src + c], gr.at[src + c], CP)]
-        add(src + c, False)
+        more = [send(gi.at[from_z + c], gi.at[from_z + c], CP), send(gr.at[from_z + c], gr.at[from_z + c], CP)]
+        add(from_z + c, False)
         for cp in more:
             cp.wait_recv()
-        add(src + 1 - c, False)
+        add(from_z + 1 - c, False)
     for cp in pieces:
         cp.wait_recv()
     tot = gb[0]
@@ -443,26 +497,31 @@
             rsb[3, 3, 0:56] = tot
         else:
             rsb[q // 4, q % 4] = acc[q // 2, :, (q % 2) * 128 : (q % 2) * 128 + 128]
+
+    st3 = []
+    for i, go in enumerate((along_z, along_x, along_y)):
+        arrived(st2[i])
+        st3.append(go(u, xx, S[i]))
+
     A, B = pl.ds(0, 56), pl.ds(56, 48)
     a4, b4 = [], []
     for d in (2, 1, 3):
-        yy, xx = lax.rem(y + d, 4), lax.rem(x + d, 4)
-        a4.append(send(rsb.at[yy, :, A], r2a.at[d - 1], YP[d - 1]))
-        b4.append(send(rsb.at[:, xx, B], r2b.at[d - 1], XP[d - 1]))
+        a4.append(send(rsb.at[ys[d], :, A], r2a.at[d - 1], YP[d - 1]))
+        b4.append(send(rsb.at[:, xs[d], B], r2b.at[d - 1], XP[d - 1]))
     for cp in a4:
         cp.wait_recv()
     t4 = rsb[y, :, 0:56, :]
     for d in range(3):
         t4 += r2a[d]
     s3a[...] = t4
-    a5 = [send(s3a.at[lax.rem(x + d, 4)], r3.at[d - 1, A], XP[d - 1]) for d in (2, 1, 3)]
+    a5 = [send(s3a.at[xs[d]], r3.at[d - 1, A], XP[d - 1]) for d in (2, 1, 3)]
     for cp in b4:
         cp.wait_recv()
     t4 = rsb[:, x, 56:104, :]
     for d in range(3):
         t4 += r2b[d]
     s3b[...] = t4
-    b5 = [send(s3b.at[lax.rem(y + d, 4)], r3.at[d - 1, B], YP[d - 1]) for d in (2, 1, 3)]
+    b5 = [send(s3b.at[ys[d]], r3.at[d - 1, B], YP[d - 1]) for d in (2, 1, 3)]
     for cp in a5:
         cp.wait_recv()
     ta = s3a[x]
@@ -475,56 +534,81 @@
         tb += r3[d, 56:104]
     done = jnp.concatenate([ta, tb, jnp.zeros((8, 128), F32)], axis=0).astype(BF)
     out[c, z, y, x] = done
-    S = (pl.ds(0, 48), pl.ds(48, 32), pl.ds(80, 32))
-    w0, w1, w2 = (out.at[c, z, y, x, s] for s in S)
-    st1 = [[send(w, w, p) for p in P] for w, P in ((w0, XP), (w1, YP), (w2, ZP))]
-    w0, w1, w2 = out.at[c, z, y, :, S[0]], out.at[c, z, :, x, S[1]], out.at[c, :, y, x, S[2]]
-    st2 = []
-    for i, (w, P) in enumerate(((w0, YP), (w1, ZP), (w2, XP))):
-        for cp in st1[i]:
+    T = (pl.ds(0, 48), pl.ds(48, 32), pl.ds(80, 32))
+    w0, w1, w2 = (out.at[c, z, y, x, s] for s in T)
+    g1 = [[send(q, q, p) for p in Q] for q, Q in ((w0, XP), (w1, YP), (w2, ZP))]
+    w0, w1, w2 = out.at[c, z, y, :, T[0]], out.at[c, z, :, x, T[1]], out.at[c, :, y, x, T[2]]
+    g2 = []
+    for i, (q, Q) in enumerate(((w0, YP), (w1, ZP), (w2, XP))):
+        for cp in g1[i]:
             cp.wait_recv()
-        st2.append([send(w, w, p) for p in P])
-    w0, w1, w2 = out.at[c, z, :, :, S[0]], out.at[c, :, :, x, S[1]], out.at[c, :, y, :, S[2]]
-    st3, last = [], []
-    for i, (w, P) in enumerate(((w0, ZP), (w1, XP), (w2, YP))):
-        for cp in st2[i]:
+        g2.append([send(q, q, p) for p in Q])
+    w0, w1, w2 = out.at[c, z, :, :, T[0]], out.at[c, :, :, x, T[1]], out.at[c, :, y, :, T[2]]
+    g3, last = [], []
+    for i, (q, Q) in enumerate(((w0, ZP), (w1, XP), (w2, YP))):
+        for cp in g2[i]:
             cp.wait_recv()
-        st3.append([send(w, w, P[d]) for d in (1, 0, 2)])
-        last.append(send(w, w, CP))
+        g3.append([send(q, q, Q[d]) for d in (1, 0, 2)])
+        last.append(send(q, q, CP))
+
+    for i in range(3):
+        arrived(st3[i])
+    unit = (lax.rem(lane // 32, 2) == 0) == (c == 0)
+    final = []
+    for zz in range(4):
+
+        def part(xi, carry):
+            for q in range(2):
+                a, b = xx[zz, xi, 2 * q], xx[zz, xi, 2 * q + 1]
+                at = pl.ds(pl.multiple_of(zz * 1024 + xi * 256 + q * 128, 128), 128)
+                recv[c, :, at] = jnp.where(unit, a, b)
+                px[:, at] = jnp.where(unit, b, a)
+            return carry
+
+        lax.fori_loop(0, 4, part, 0)
+        span = pl.ds(zz * 1024, 1024)
+        final.append(send(px.at[:, span], recv.at[c, :, span], CP))
+
     for i in range(3):
         for j, d in ((1, 1), (2, 3), (0, 2)):
-            st3[i][j].wait_recv()
+            g3[i][j].wait_recv()
             if i == 0:
-                w = out.at[c, lax.rem(z - d + 4, 4), :, :, S[0]]
+                q = out.at[c, lax.rem(z - d + 4, 4), :, :, T[0]]
             elif i == 1:
-                w = out.at[c, :, :, lax.rem(x - d + 4, 4), S[1]]
+                q = out.at[c, :, :, lax.rem(x - d + 4, 4), T[1]]
             else:
-                w = out.at[c, :, lax.rem(y - d + 4, 4), :, S[2]]
-            last.append(send(w, w, CP))
-    for cp in last:
+                q = out.at[c, :, lax.rem(y - d + 4, 4), :, T[2]]
+            last.append(send(q, q, CP))
+    for cp in last + final:
         cp.wait_recv()
     for cp in sent:
         cp.wait_send()
 
 
-def reduce_all(rows, rel, bpart):
+def exchange(rows, rel, bpart, pos, orow, grads):
     sem = pltpu.SemaphoreType.DMA
     v = pltpu.VMEM
+    big = (4, 4, 4, HALF, 128)
     return pl.pallas_call(
-        reduce_kernel,
-        out_shape=jax.ShapeDtypeStruct((2, 4, 4, 4, 112, 128), BF),
-        in_specs=[VM] * 3,
-        out_specs=VM,
+        exchange_kernel,
+        out_shape=(
+            jax.ShapeDtypeStruct((2, 4, 4, 4, 112, 128), BF),
+            jax.ShapeDtypeStruct((2, HALF, 4096), BF),
+        ),
+        in_specs=[VM] * 6,
+        out_specs=(VM, VM),
         scratch_shapes=[
             v((8, 224, TRIP), BF), v((8, 1, TRIP), jnp.int32), v((8, 56, 128), F32), v((8, 104, 256), F32),
             v((4, 4, 104, 128), F32), v((3, 4, 56, 128), F32), v((3, 4, 48, 128), F32),
             v((4, 56, 128), F32), v((4, 48, 128), F32), v((3, 104, 128), F32),
-            sem((80,)), sem((80,)), sem((3,)),
+            v((2 * HALF, 2 * TRIP), BF), v((256, 2 * TRIP), BF), v((2, 16, HALF, 256), BF), v((16, HALF, 256), BF),
+            v(big, BF), v(big, BF), v(big, BF), v(big, BF), v((HALF, 4096), BF),
+            sem((160,)), sem((160,)), sem((16,)),
         ],
-        compiler_params=pltpu.CompilerParams(collective_id=1, has_side_effects=True, vmem_limit_bytes=40 * 2**20),
+        compiler_params=pltpu.CompilerParams(collective_id=1, has_side_effects=True, vmem_limit_bytes=56 * 2**20),
         cost_estimate=pl.CostEstimate(flops=8 * 10**10, bytes_accessed=10**7, transcendentals=0),
-        name="reduce",
-    )(rows, rel, bpart)
+        name="exchange",
+    )(rows, rel, bpart, pos, orow, grads)
 
 
 def unpack_kernel(tiles, coef_out, bases_out):
@@ -558,9 +642,7 @@
     own_neg, grads, rows, bases_part, pos = score(
         head_emb.T, tail_emb.T, rel, owners.T, neg_rows, bases.T, coef.T, entities.T
     )
-    packed = pack(pos, owner_rows.T, grads)
-    recv = lax.all_to_all(packed, ("grp", "dev"), split_axis=0, concat_axis=0, tiled=True)
-    tiles = reduce_all(rows, rel, bases_part)
+    tiles, recv = exchange(rows, rel, bases_part, pos, owner_rows.T, grads)
     coef_grad, bases_grad = unpack(tiles)
     ent_grad = place(recv, own_neg, neg_rows)
     return ent_grad.T, coef_grad.T, bases_grad.T

time: 218 us -> 185 us (0.85)
  Pallas kernels: 203 us -> 182 us
  starting transfers between devices: 8.68 us -> 0 us
  local copies, waits for them, and re-layouts: 4.15 us -> 1.97 us
    pallas_call x2 -> x1, Pallas kernels: 121 us -> 103 us  [exchange(): pl.pallas_call(exchange_kernel, out_shape=(jax.ShapeDtypeStruct((2, 4, 4,...]
    all_to_all x1 -> x0, starting transfers between devices: 8.68 us -> none  [per_device(): lax.all_to_all(packed, ('grp', 'dev'), split_axis=0, concat_axis=0, tiled...]
    pallas_call x1, Pallas kernels: 22.9 us -> 20 us  [place(): pl.pallas_call(place_kernel, grid=(16,), out_shape=jax.ShapeDtypeStruct((...]
    unnamed x18 -> x8, local copies, waits for them, and re-layouts: 4.15 us -> 1.97 us
  transfers between devices with their start and end apart: 1 -> 0, of which waited for: 0 -> 0; matrix products, arithmetic and copies ran while one was open for 0% -> 0% of each run, Pallas kernels for 52% -> 0%
where the time goes in v2:
time: 185 us
  Pallas kernels  182 us (98%)
  local copies, waits for them, and re-layouts  1.97 us (1%)
    pallas_call x1, Pallas kernels, exchange(): pl.pallas_call(exchange_kernel, out_shape=(jax.ShapeDtypeStruct((2, 4, 4,...  103 us
    pallas_call x1, Pallas kernels, score(): pl.pallas_call(score_kernel, out_shape=(jax.ShapeDtypeStruct((D, NEG), F3...  55.2 us
    pallas_call x1, Pallas kernels, place(): pl.pallas_call(place_kernel, grid=(16,), out_shape=jax.ShapeDtypeStruct((...  20 us
    pallas_call x1, Pallas kernels, unpack(): pl.pallas_call(unpack_kernel, grid=(8,), out_shape=(jax.ShapeDtypeStruct(...  4 us

profile of v2, /device:TPU:1, one launch (start us, length us, event | category | flops | bytes accessed | tf_op | source)
XLA Modules:
  0.0 185.0 jit_solution(919090050496797695)
XLA Ops:
  0.6 55.2 %score.1 = (f32[400,128]{1,0:T(8,128)}, bf16[2,400,1024]{2,1,0:T(8,128)(2,1)}, bf16[224,1024]{1,0:T(8,128)(2,1)}, f32[448,128]{1,0:T(8,128)}, s32[2,1024]{1,0:T(2,128)}) custom-call(bf16[400,1024]{1,0:T(8,128)(2,1)} %bitcast.14, bf16[400,1024]{1,0:T(8,128)(2,1)} %bitcast.15, s32[1,1024]{1,0:T(1,128)} %bitcast.20, s32[2,1024]{1,0:T(2,128)} %bitcast.18, ...), custom_call_target="tpu_custom_call" | custom-call | flops 99999997952 | bytes 10000000 | tf_op jit(solution)/shard_map/score/pallas_call | solution.py:251
  55.8 0.0 copy-start.1
  55.8 0.0 copy-start.3
  55.9 103.1 %exchange.1 = (bf16[2,4,4,4,112,128]{5,4,3,2,1,0:T(8,128)(2,1)}, bf16[2,208,4096]{2,1,0:T(8,128)(2,1)}) custom-call(bf16[224,1024]{1,0:T(8,128)(2,1)} %get-tuple-element.12.rows, s32[1,1024]{1,0:T(1,128)} %bitcast.21, f32[448,128]{1,0:T(8,128)} %get-tuple-element.13.bpart, s32[2,1024]{1,0:T(2,128)} %get-tuple-element.14.pos, s32[2,1024]{1,0:T(2,128)} %bitcast.19, ...), custom_call_target="tpu_custom_call" | custom-call | flops 80000000000 | bytes 10000000 | tf_op jit(solution)/shard_map/exchange/pallas_call | solution.py:592
  159.0 0.0 copy-done.1
  159.0 0.0 copy-done.3
  159.0 0.0 copy-start.2
  159.0 2.0 %copy-done.2 = bf16[2,208,4096]{2,1,0:T(8,128)(2,1)S(1)} copy-done((bf16[2,208,4096]{2,1,0:T(8,128)(2,1)S(1)}, bf16[2,208,4096]{2,1,0:T(8,128)(2,1)}, u32[]{:S(2)}) %copy-start.2) | copy-done | bytes 3407896
  161.0 0.0 copy-start
  161.0 20.0 %place.1 = f32[400,4096]{1,0:T(8,128)} custom-call(bf16[2,208,4096]{2,1,0:T(8,128)(2,1)S(1)} %copy-done.2, f32[400,128]{1,0:T(8,128)S(1)} %copy-done.3, s32[1,128]{1,0:T(1,128)S(1)} %copy-done.1), custom_call_target="tpu_custom_call" | custom-call | flops 14000000000 | bytes 11000000 | tf_op jit(solution)/shard_map/place/pallas_call | solution.py:303
  181.0 0.0 copy-done
  181.0 4.0 %unpack.1 = (f32[100,14824]{1,0:T(8,128)}, f32[400,100]{1,0:T(8,128)}) custom-call(bf16[2,4,4,4,112,128]{5,4,3,2,1,0:T(8,128)(2,1)S(1)} %copy-done), custom_call_target="tpu_custom_call" | custom-call | tf_op jit(solution)/shard_map/unpack/pallas_call | solution.py:629
Async XLA Ops:
  55.8 103.1 %copy-start.1 = (s32[1,128]{1,0:T(1,128)S(1)}, s32[1,128]{1,0:T(1,128)}, u32[]{:S(2)}) copy-start(s32[1,128]{1,0:T(1,128)} %negr.3) | copy-start | bytes 1540
  55.8 103.1 %copy-start.3 = (f32[400,128]{1,0:T(8,128)S(1)}, f32[400,128]{1,0:T(8,128)}, u32[]{:S(2)}) copy-start(f32[400,128]{1,0:T(8,128)} %get-tuple-element.17.own_neg) | copy-start | bytes 614404
  159.0 2.0 %copy-start.2 = (bf16[2,208,4096]{2,1,0:T(8,128)(2,1)S(1)}, bf16[2,208,4096]{2,1,0:T(8,128)(2,1)}, u32[]{:S(2)}) copy-start(bf16[2,208,4096]{2,1,0:T(8,128)(2,1)} %get-tuple-element.16.recv) | copy-start | bytes 10223620
  161.0 20.0 %copy-start = (bf16[2,4,4,4,112,128]{5,4,3,2,1,0:T(8,128)(2,1)S(1)}, bf16[2,4,4,4,112,128]{5,4,3,2,1,0:T(8,128)(2,1)}, u32[]{:S(2)}) copy-start(bf16[2,4,4,4,112,128]{5,4,3,2,1,0:T(8,128)(2,1)} %get-tuple-element.18.tiles) | copy-start | bytes 11010052

commit v3 on v2

--- a/solution.py
+++ b/solution.py
@@ -292,21 +292,24 @@
         rt[0:D, 4096 + NEG : WIDE] = (n - first.astype(F32)).astype(BF)
         ids[:, 4096 : 4096 + NEG] = negr[...]
         ids[:, 4096 + NEG : WIDE] = negr[...]
-        low[...] = spread(ids[...] & 255, 256)
-
-    one = low[...] * equals(lax.shift_right_logical(ids[...], 8), step)
-    out[...] = dot(rt[0:D, :], one, 1, 1)
+        for q in range(WIDE // 256):
+            at = q * 256
+            low[at : at + 256, :] = spread(ids[:, at : at + 256] & 255, 256).T
+
+    for q in range(2):
+        keep = equals(lax.shift_right_logical(ids[...], 8), step * 2 + q)
+        out[:, q * 256 : (q + 1) * 256] = dot(rt[...] * keep, low[...])
 
 
 def place(recv, own_neg, negr):
     whole = lambda *s: pl.BlockSpec(s, lambda i: (0,) * len(s))
     return pl.pallas_call(
         place_kernel,
-        grid=(16,),
+        grid=(8,),
         out_shape=jax.ShapeDtypeStruct((D, ENT), F32),
         in_specs=[whole(2, HALF, 4096), whole(D, NEG), whole(1, NEG)],
-        out_specs=pl.BlockSpec((D, 256), lambda i: (0, i)),
-        scratch_shapes=[pltpu.VMEM((D, WIDE), BF), pltpu.VMEM((256, WIDE), BF), pltpu.VMEM((1, WIDE), jnp.int32)],
+        out_specs=pl.BlockSpec((D, 512), lambda i: (0, i)),
+        scratch_shapes=[pltpu.VMEM((D, WIDE), BF), pltpu.VMEM((WIDE, 256), BF), pltpu.VMEM((1, WIDE), jnp.int32)],
         compiler_params=pltpu.CompilerParams(vmem_limit_bytes=40 * 2**20),
         cost_estimate=pl.CostEstimate(flops=14 * 10**9, bytes_accessed=11 * 10**6, transcendentals=0),
         name="place",
@@ -378,7 +381,18 @@
     for cp in kept:
         cp.wait()
     pl.semaphore_wait(bar, 13)
-    first = [[send(rel, gi.at[own], ZP[d]), send(rows, gr.at[own], ZP[d])] for d in (0, 2, 1)]
+    first = [[send(rel, gi.at[own], p), send(rows, gr.at[own], p)] for p in (ZP[0], ZP[2])]
+    zm, zp = zs[3] * 2 + c, zs[1] * 2 + c
+    HI, LO = pl.ds(0, LOROW), pl.ds(LOROW, LOROW)
+
+    def pass_on():
+        for cp in first[0]:
+            cp.wait_recv()
+        away = [send(gi.at[zm], gi.at[zm], ZP[0]), send(gr.at[zm, HI], gr.at[zm, HI], ZP[0])]
+        for cp in first[1]:
+            cp.wait_recv()
+        return away + [send(gr.at[zp, LO], gr.at[zp, LO], ZP[2])]
+
     near = [send(rel, gi.at[own], CP), send(rows, gr.at[own], CP)]
     pieces = []
 
@@ -431,6 +445,8 @@
         for d in (1, 3, 2):
             st1[0].append(send(w.at[zz, xs[d], :, S[0]], v.at[zz, x, :, S[0]], XP[d - 1]))
             st1[1].append(send(w.at[zz, :, ys[d], S[1]], v.at[zz, :, y, S[1]], YP[d - 1]))
+        if gp == 2:
+            away = pass_on()
         if gp < 3:
             st1[2].append(send(w.at[zz, :, :, S[2]], v.at[z, :, :, S[2]], ZP[gp]))
     st1[0].append(keep(w.at[:, x, :, S[0]], v.at[:, x, :, S[0]]))
@@ -478,9 +494,10 @@
         st2.append(go(v, u, S[i]))
 
     for i, d in enumerate((1, 3, 2)):
-        from_z = lax.rem(z - d + 4, 4) * 2
-        for cp in first[i]:
-            cp.wait_recv()
+        from_z = zs[4 - d] * 2
+        if i == 2:
+            for cp in away:
+                cp.wait_recv()
         more = [send(gi.at[from_z + c], gi.at[from_z + c], CP), send(gr.at[from_z + c], gr.at[from_z + c], CP)]
         add(from_z + c, False)
         for cp in more:
@@ -534,18 +551,16 @@
         tb += r3[d, 56:104]
     done = jnp.concatenate([ta, tb, jnp.zeros((8, 128), F32)], axis=0).astype(BF)
     out[c, z, y, x] = done
-    T = (pl.ds(0, 48), pl.ds(48, 32), pl.ds(80, 32))
-    w0, w1, w2 = (out.at[c, z, y, x, s] for s in T)
-    g1 = [[send(q, q, p) for p in Q] for q, Q in ((w0, XP), (w1, YP), (w2, ZP))]
-    w0, w1, w2 = out.at[c, z, y, :, T[0]], out.at[c, z, :, x, T[1]], out.at[c, :, y, x, T[2]]
-    g2 = []
-    for i, (q, Q) in enumerate(((w0, YP), (w1, ZP), (w2, XP))):
-        for cp in g1[i]:
-            cp.wait_recv()
-        g2.append([send(q, q, p) for p in Q])
-    w0, w1, w2 = out.at[c, z, :, :, T[0]], out.at[c, :, :, x, T[1]], out.at[c, :, y, :, T[2]]
+    T = (pl.ds(0, 64), pl.ds(64, 48))
+    q = out.at[c, z, y, x]
+    g1 = [send(q, q, p) for p in ZP]
+    for cp in g1:
+        cp.wait_recv()
+    w0, w1 = out.at[c, :, y, x, T[0]], out.at[c, :, y, x, T[1]]
+    g2 = [[send(q, q, p) for p in Q] for q, Q in ((w0, XP), (w1, YP))]
+    w0, w1 = out.at[c, :, y, :, T[0]], out.at[c, :, :, x, T[1]]
     g3, last = [], []
-    for i, (q, Q) in enumerate(((w0, ZP), (w1, XP), (w2, YP))):
+    for i, (q, Q) in enumerate(((w0, YP), (w1, XP))):
         for cp in g2[i]:
             cp.wait_recv()
         g3.append([send(q, q, Q[d]) for d in (1, 0, 2)])
@@ -569,15 +584,13 @@
         span = pl.ds(zz * 1024, 1024)
         final.append(send(px.at[:, span], recv.at[c, :, span], CP))
 
-    for i in range(3):
-        for j, d in ((1, 1), (2, 3), (0, 2)):
+    for j, d in ((1, 1), (2, 3), (0, 2)):
+        for i in range(2):
             g3[i][j].wait_recv()
             if i == 0:
-                q = out.at[c, lax.rem(z - d + 4, 4), :, :, T[0]]
-            elif i == 1:
-                q = out.at[c, :, :, lax.rem(x - d + 4, 4), T[1]]
+                q = out.at[c, :, ys[4 - d], :, T[0]]
             else:
-                q = out.at[c, :, lax.rem(y - d + 4, 4), :, T[2]]
+                q = out.at[c, :, :, xs[4 - d], T[1]]
             last.append(send(q, q, CP))
     for cp in last + final:
         cp.wait_recv()

time: 185 us -> 180 us (0.973)
  Pallas kernels: 182 us -> 177 us
    pallas_call x1, Pallas kernels: 103 us -> 100 us  [exchange(): pl.pallas_call(exchange_kernel, out_shape=(jax.ShapeDtypeStruct((2, 4, 4,...]
    pallas_call x1, Pallas kernels: 20 us -> 17.5 us  [place(): pl.pallas_call(place_kernel, grid=(8,), out_shape=jax.ShapeDtypeStruct((D...]
where the time goes in v3:
time: 180 us
  Pallas kernels  177 us (98%)
  local copies, waits for them, and re-layouts  1.97 us (1%)
    pallas_call x1, Pallas kernels, exchange(): pl.pallas_call(exchange_kernel, out_shape=(jax.ShapeDtypeStruct((2, 4, 4,...  100 us
    pallas_call x1, Pallas kernels, score(): pl.pallas_call(score_kernel, out_shape=(jax.ShapeDtypeStruct((D, NEG), F3...  55.2 us
    pallas_call x1, Pallas kernels, place(): pl.pallas_call(place_kernel, grid=(8,), out_shape=jax.ShapeDtypeStruct((D...  17.5 us
    pallas_call x1, Pallas kernels, unpack(): pl.pallas_call(unpack_kernel, grid=(8,), out_shape=(jax.ShapeDtypeStruct(...  4 us

profile of v3, /device:TPU:1, one launch (start us, length us, event | category | flops | bytes accessed | tf_op | source)
XLA Modules:
  0.0 179.8 jit_solution(17856318752906528071)
XLA Ops:
  0.6 55.2 %score.1 = (f32[400,128]{1,0:T(8,128)}, bf16[2,400,1024]{2,1,0:T(8,128)(2,1)}, bf16[224,1024]{1,0:T(8,128)(2,1)}, f32[448,128]{1,0:T(8,128)}, s32[2,1024]{1,0:T(2,128)}) custom-call(bf16[400,1024]{1,0:T(8,128)(2,1)} %bitcast.14, bf16[400,1024]{1,0:T(8,128)(2,1)} %bitcast.15, s32[1,1024]{1,0:T(1,128)} %bitcast.20, s32[2,1024]{1,0:T(2,128)} %bitcast.18, ...), custom_call_target="tpu_custom_call" | custom-call | flops 99999997952 | bytes 10000000 | tf_op jit(solution)/shard_map/score/pallas_call | solution.py:251
  55.8 0.0 copy-start.1
  55.8 0.0 copy-start.3
  55.9 100.5 %exchange.1 = (bf16[2,4,4,4,112,128]{5,4,3,2,1,0:T(8,128)(2,1)}, bf16[2,208,4096]{2,1,0:T(8,128)(2,1)}) custom-call(bf16[224,1024]{1,0:T(8,128)(2,1)} %get-tuple-element.12.rows, s32[1,1024]{1,0:T(1,128)} %bitcast.21, f32[448,128]{1,0:T(8,128)} %get-tuple-element.13.bpart, s32[2,1024]{1,0:T(2,128)} %get-tuple-element.14.pos, s32[2,1024]{1,0:T(2,128)} %bitcast.19, ...), custom_call_target="tpu_custom_call" | custom-call | flops 80000000000 | bytes 10000000 | tf_op jit(solution)/shard_map/exchange/pallas_call | solution.py:605
  156.3 0.0 copy-done.1
  156.3 0.0 copy-done.3
  156.4 0.0 copy-start.2
  156.4 2.0 %copy-done.2 = bf16[2,208,4096]{2,1,0:T(8,128)(2,1)S(1)} copy-done((bf16[2,208,4096]{2,1,0:T(8,128)(2,1)S(1)}, bf16[2,208,4096]{2,1,0:T(8,128)(2,1)}, u32[]{:S(2)}) %copy-start.2) | copy-done | bytes 3407896
  158.3 0.0 copy-start
  158.3 17.5 %place.1 = f32[400,4096]{1,0:T(8,128)} custom-call(bf16[2,208,4096]{2,1,0:T(8,128)(2,1)S(1)} %copy-done.2, f32[400,128]{1,0:T(8,128)S(1)} %copy-done.3, s32[1,128]{1,0:T(1,128)S(1)} %copy-done.1), custom_call_target="tpu_custom_call" | custom-call | flops 14000000000 | bytes 11000000 | tf_op jit(solution)/shard_map/place/pallas_call | solution.py:306
  175.8 0.0 copy-done
  175.8 4.0 %unpack.1 = (f32[100,14824]{1,0:T(8,128)}, f32[400,100]{1,0:T(8,128)}) custom-call(bf16[2,4,4,4,112,128]{5,4,3,2,1,0:T(8,128)(2,1)S(1)} %copy-done), custom_call_target="tpu_custom_call" | custom-call | tf_op jit(solution)/shard_map/unpack/pallas_call | solution.py:642
Async XLA Ops:
  55.8 100.5 %copy-start.1 = (s32[1,128]{1,0:T(1,128)S(1)}, s32[1,128]{1,0:T(1,128)}, u32[]{:S(2)}) copy-start(s32[1,128]{1,0:T(1,128)} %negr.3) | copy-start | bytes 1540
  55.8 100.5 %copy-start.3 = (f32[400,128]{1,0:T(8,128)S(1)}, f32[400,128]{1,0:T(8,128)}, u32[]{:S(2)}) copy-start(f32[400,128]{1,0:T(8,128)} %get-tuple-element.17.own_neg) | copy-start | bytes 614404
  156.4 2.0 %copy-start.2 = (bf16[2,208,4096]{2,1,0:T(8,128)(2,1)S(1)}, bf16[2,208,4096]{2,1,0:T(8,128)(2,1)}, u32[]{:S(2)}) copy-start(bf16[2,208,4096]{2,1,0:T(8,128)(2,1)} %get-tuple-element.16.recv) | copy-start | bytes 10223620
  158.3 17.5 %copy-start = (bf16[2,4,4,4,112,128]{5,4,3,2,1,0:T(8,128)(2,1)S(1)}, bf16[2,4,4,4,112,128]{5,4,3,2,1,0:T(8,128)(2,1)}, u32[]{:S(2)}) copy-start(bf16[2,4,4,4,112,128]{5,4,3,2,1,0:T(8,128)(2,1)} %get-tuple-element.18.tiles) | copy-start | bytes 11010052

commit v4 on v3

--- a/solution.py
+++ b/solution.py
@@ -515,16 +515,16 @@
         else:
             rsb[q // 4, q % 4] = acc[q // 2, :, (q % 2) * 128 : (q % 2) * 128 + 128]
 
-    st3 = []
-    for i, go in enumerate((along_z, along_x, along_y)):
-        arrived(st2[i])
-        st3.append(go(u, xx, S[i]))
-
     A, B = pl.ds(0, 56), pl.ds(56, 48)
     a4, b4 = [], []
     for d in (2, 1, 3):
         a4.append(send(rsb.at[ys[d], :, A], r2a.at[d - 1], YP[d - 1]))
         b4.append(send(rsb.at[:, xs[d], B], r2b.at[d - 1], XP[d - 1]))
+    st3 = []
+    for i, go in enumerate((along_z, along_x, along_y)):
+        arrived(st2[i])
+        st3.append(go(u, xx, S[i]))
+
     for cp in a4:
         cp.wait_recv()
     t4 = rsb[y, :, 0:56, :]

time: 180 us -> 177 us (0.983)
  Pallas kernels: 177 us -> 174 us
    pallas_call x1, Pallas kernels: 100 us -> 97.2 us  [exchange(): pl.pallas_call(exchange_kernel, out_shape=(jax.ShapeDtypeStruct((2, 4, 4,...]
where the time goes in v4:
time: 177 us
  Pallas kernels  174 us (98%)
  local copies, waits for them, and re-layouts  1.97 us (1%)
    pallas_call x1, Pallas kernels, exchange(): pl.pallas_call(exchange_kernel, out_shape=(jax.ShapeDtypeStruct((2, 4, 4,...  97.2 us
    pallas_call x1, Pallas kernels, score(): pl.pallas_call(score_kernel, out_shape=(jax.ShapeDtypeStruct((D, NEG), F3...  55.2 us
    pallas_call x1, Pallas kernels, place(): pl.pallas_call(place_kernel, grid=(8,), out_shape=jax.ShapeDtypeStruct((D...  17.5 us
    pallas_call x1, Pallas kernels, unpack(): pl.pallas_call(unpack_kernel, grid=(8,), out_shape=(jax.ShapeDtypeStruct(...  4 us

profile of v4, /device:TPU:1, one launch (start us, length us, event | category | flops | bytes accessed | tf_op | source)
XLA Modules:
  0.0 176.5 jit_solution(12853021574371867162)
XLA Ops:
  0.6 55.2 %score.1 = (f32[400,128]{1,0:T(8,128)}, bf16[2,400,1024]{2,1,0:T(8,128)(2,1)}, bf16[224,1024]{1,0:T(8,128)(2,1)}, f32[448,128]{1,0:T(8,128)}, s32[2,1024]{1,0:T(2,128)}) custom-call(bf16[400,1024]{1,0:T(8,128)(2,1)} %bitcast.14, bf16[400,1024]{1,0:T(8,128)(2,1)} %bitcast.15, s32[1,1024]{1,0:T(1,128)} %bitcast.20, s32[2,1024]{1,0:T(2,128)} %bitcast.18, ...), custom_call_target="tpu_custom_call" | custom-call | flops 99999997952 | bytes 10000000 | tf_op jit(solution)/shard_map/score/pallas_call | solution.py:251
  55.8 0.0 copy-start.1
  55.8 0.0 copy-start.3
  55.9 97.2 %exchange.1 = (bf16[2,4,4,4,112,128]{5,4,3,2,1,0:T(8,128)(2,1)}, bf16[2,208,4096]{2,1,0:T(8,128)(2,1)}) custom-call(bf16[224,1024]{1,0:T(8,128)(2,1)} %get-tuple-element.12.rows, s32[1,1024]{1,0:T(1,128)} %bitcast.21, f32[448,128]{1,0:T(8,128)} %get-tuple-element.13.bpart, s32[2,1024]{1,0:T(2,128)} %get-tuple-element.14.pos, s32[2,1024]{1,0:T(2,128)} %bitcast.19, ...), custom_call_target="tpu_custom_call" | custom-call | flops 80000000000 | bytes 10000000 | tf_op jit(solution)/shard_map/exchange/pallas_call | solution.py:605
  153.0 0.0 copy-done.1
  153.0 0.0 copy-done.3
  153.1 0.0 copy-start.2
  153.1 2.0 %copy-done.2 = bf16[2,208,4096]{2,1,0:T(8,128)(2,1)S(1)} copy-done((bf16[2,208,4096]{2,1,0:T(8,128)(2,1)S(1)}, bf16[2,208,4096]{2,1,0:T(8,128)(2,1)}, u32[]{:S(2)}) %copy-start.2) | copy-done | bytes 3407896
  155.0 0.0 copy-start
  155.0 17.5 %place.1 = f32[400,4096]{1,0:T(8,128)} custom-call(bf16[2,208,4096]{2,1,0:T(8,128)(2,1)S(1)} %copy-done.2, f32[400,128]{1,0:T(8,128)S(1)} %copy-done.3, s32[1,128]{1,0:T(1,128)S(1)} %copy-done.1), custom_call_target="tpu_custom_call" | custom-call | flops 14000000000 | bytes 11000000 | tf_op jit(solution)/shard_map/place/pallas_call | solution.py:306
  172.5 0.0 copy-done
  172.5 4.0 %unpack.1 = (f32[100,14824]{1,0:T(8,128)}, f32[400,100]{1,0:T(8,128)}) custom-call(bf16[2,4,4,4,112,128]{5,4,3,2,1,0:T(8,128)(2,1)S(1)} %copy-done), custom_call_target="tpu_custom_call" | custom-call | tf_op jit(solution)/shard_map/unpack/pallas_call | solution.py:642
Async XLA Ops:
  55.8 97.2 %copy-start.1 = (s32[1,128]{1,0:T(1,128)S(1)}, s32[1,128]{1,0:T(1,128)}, u32[]{:S(2)}) copy-start(s32[1,128]{1,0:T(1,128)} %negr.3) | copy-start | bytes 1540
  55.8 97.2 %copy-start.3 = (f32[400,128]{1,0:T(8,128)S(1)}, f32[400,128]{1,0:T(8,128)}, u32[]{:S(2)}) copy-start(f32[400,128]{1,0:T(8,128)} %get-tuple-element.17.own_neg) | copy-start | bytes 614404
  153.1 2.0 %copy-start.2 = (bf16[2,208,4096]{2,1,0:T(8,128)(2,1)S(1)}, bf16[2,208,4096]{2,1,0:T(8,128)(2,1)}, u32[]{:S(2)}) copy-start(bf16[2,208,4096]{2,1,0:T(8,128)(2,1)} %get-tuple-element.16.recv) | copy-start | bytes 10223620
  155.0 17.5 %copy-start = (bf16[2,4,4,4,112,128]{5,4,3,2,1,0:T(8,128)(2,1)S(1)}, bf16[2,4,4,4,112,128]{5,4,3,2,1,0:T(8,128)(2,1)}, u32[]{:S(2)}) copy-start(bf16[2,4,4,4,112,128]{5,4,3,2,1,0:T(8,128)(2,1)} %get-tuple-element.18.tiles) | copy-start | bytes 11010052
